TPU v7x, 32 devices: a whole 2x2x4 slice. The times are simulated.
32 devices in a mesh: tiles: 2 (over y), disp: 4 (over z), rows: 2 (over x), cols: 2 (over core).
Axes of the slice: x: 2, y: 2, z: 4, core: 2. Of those that a mesh axis runs over, the one named last changes fastest.
Arguments:
- left_feat: bfloat16 [4, 256, 320], P(('tiles', 'rows'), ('cols', 'disp')), parts along dimension 0, may hold values from -64 to 64
- right_feat: bfloat16 [4, 256, 320], P(('tiles', 'rows'), ('cols', 'disp')), parts along dimension 0, may hold values from -64 to 64
- conv_first: bfloat16 [27, 32, 40], replicated, may hold values from -0.1875 to 0.1875
- conv_mid: bfloat16 [2, 27, 32, 32], replicated, may hold values from -0.21875 to 0.21875
- conv_last: bfloat16 [27, 1, 32], replicated, may hold values from -3 to 3
Outputs:
- estimate: float32 [4, 256], P(('tiles', 'rows'), ('cols', 'disp')), parts along dimension 0
There are 2 independent parts, one for each index of `tiles`. A program takes and returns all parts, laid end to end along the dimension named above; an argument that names none is the same for every part. Nothing has to cross between parts.
All inputs are finite; a program needn't handle non-finite values.
Results may differ from a plain program's by a relative error of at most 0.012.
The roundings to bfloat16 on the way count: a program that leaves them out, or rounds other values in their place, can miss the bound.
Values may be sent and summed in bfloat16 or wider, within the bound.
No kernel may reach another device: no remote copies, remote signals or barrier semaphores. Data moves between devices by JAX's collectives and lax.ppermute only.
A program may use at most 64 MiB of HBM per device.

v0:
```python
import jax
import jax.numpy as jnp
from jax import lax
from jax.sharding import PartitionSpec as P

MID = 2
DDEV = 16


def extended_2(block, sides, width):
    for axis, dim in sides:
        count = lax.axis_size(axis)
        forward = [(i, i + 1) for i in range(count - 1)]
        backward = [(target, source) for source, target in forward]
        low = lax.ppermute(
            lax.slice_in_dim(block, block.shape[dim] - width, None, axis=dim), axis, forward
        )
        high = lax.ppermute(lax.slice_in_dim(block, 0, width, axis=dim), axis, backward)
        block = jnp.concatenate([low, block, high], axis=dim)
    return block


def passed_along(x, axis, by):
    peers = lax.axis_size(axis)
    pairs = [(i, i + by) for i in range(peers) if 0 <= i + by < peers]
    return lax.ppermute(x, axis, pairs)


def combined_all(part, axis, combine):
    gathered = jax.tree.map(lambda a: lax.all_gather(a, axis), part)

    def take(source):
        return jax.tree.map(lambda a: lax.dynamic_index_in_dim(a, source, 0, False), gathered)

    return lax.fori_loop(
        1, lax.axis_size(axis), lambda source, state: combine(state, take(source)), take(0)
    )


def correlate(left_full, extended, groups, first_disp, count, total_disp):
    rows_here, width_here, channels = left_full.shape
    group_size = channels // groups
    left_groups = left_full.reshape(rows_here, width_here, groups, group_size)

    def single(offset):
        disp_value = first_disp + offset
        shifted = lax.dynamic_slice_in_dim(extended, 2 * width_here - disp_value, width_here, 1)
        right_groups = shifted.reshape(rows_here, width_here, groups, group_size)
        corr = (
            jnp.einsum(
                "hwgc,hwgc->ghw", left_groups, right_groups, preferred_element_type=jnp.float32
            )
            / group_size
        )
        inside = (disp_value >= 0) & (disp_value < total_disp)
        return jnp.where(inside, corr, 0.0).astype(jnp.bfloat16)

    return lax.map(single, jnp.arange(count, dtype=jnp.int32))


def convolve(padded, kernel):
    depth_out = padded.shape[0] - 2
    in_chans = padded.shape[1]
    rows_out = padded.shape[2] - 2
    cols_out = padded.shape[3] - 2
    out_chans = kernel.shape[1]
    columns = jnp.concatenate(
        [
            padded[:, :, row_tap : row_tap + rows_out, col_tap : col_tap + cols_out]
            for row_tap in range(3)
            for col_tap in range(3)
        ],
        axis=1,
    )
    flat = columns.reshape(depth_out + 2, 9 * in_chans, rows_out * cols_out)
    summed = jnp.zeros((depth_out, out_chans, rows_out * cols_out), jnp.float32)
    for disp_tap in range(3):
        taps = (
            jnp.transpose(kernel[9 * disp_tap : 9 * disp_tap + 9], (1, 0, 2))
            .reshape(out_chans, 9 * in_chans)
            .astype(flat.dtype)
        )
        summed = summed + jnp.einsum(
            "ok,dkn->don",
            taps,
            flat[disp_tap : disp_tap + depth_out],
            preferred_element_type=jnp.float32,
            precision=lax.Precision.HIGHEST,
        )
    return summed.reshape(depth_out, out_chans, rows_out, cols_out)


def widen(hidden):
    return extended_2(hidden, (("disp", 0), ("rows", 2), ("cols", 3)), 1)


def combine_parts(earlier, later):
    highest = jnp.maximum(earlier[0], later[0])
    scale_one = jnp.exp(earlier[0] - highest)
    scale_two = jnp.exp(later[0] - highest)
    return (
        highest,
        earlier[1] * scale_one + later[1] * scale_two,
        earlier[2] * scale_one + later[2] * scale_two,
    )


def shards(left_feat, right_feat, conv_first, conv_mid, conv_last):
    piece_width = left_feat.shape[1]
    groups = conv_first.shape[2]
    disp_count = lax.axis_size("disp")
    depth_here = DDEV
    total_disp = depth_here * disp_count
    first_disp = lax.axis_index("disp") * depth_here
    left_full, right_full = (
        lax.all_gather(left_feat, "disp", axis=1, tiled=True),
        lax.all_gather(right_feat, "disp", axis=1, tiled=True),
    )
    prior_full = passed_along(right_full, "cols", 1)
    extended = jnp.concatenate([jnp.zeros_like(right_full), prior_full, right_full], axis=1)
    volume = correlate(left_full, extended, groups, first_disp, depth_here, total_disp)
    padded = extended_2(volume, (("disp", 0), ("rows", 2), ("cols", 3)), 1)
    hidden = jax.nn.relu(convolve(padded, conv_first))
    for layer in range(MID):
        hidden = jax.nn.relu(convolve(widen(hidden), conv_mid[layer]))
    cost_cube = convolve(widen(hidden), conv_last)[:, 0]
    levels = (
        (first_disp + jnp.arange(depth_here, dtype=jnp.int32)).astype(jnp.float32) / total_disp
    )[:, None, None]
    local_high = jnp.max(cost_cube, axis=0)
    weights = jnp.exp(cost_cube - local_high[None])
    merged = combined_all(
        (local_high, jnp.sum(weights, axis=0), jnp.sum(weights * levels, axis=0)),
        "disp",
        combine_parts,
    )
    whole_row = merged[2] / merged[1]
    return lax.dynamic_slice_in_dim(whole_row, lax.axis_index("disp") * piece_width, piece_width, 1)


def solution(mesh):
    return jax.shard_map(
        shards,
        mesh=mesh,
        in_specs=(
            P(("tiles", "rows"), ("cols", "disp"), None),
            P(("tiles", "rows"), ("cols", "disp"), None),
            P(),
            P(),
            P(),
        ),
        out_specs=P(("tiles", "rows"), ("cols", "disp")),
        check_vma=False,
    )
```

profile of v0, /device:TPU:0, one launch (start us, length us, event | category | flops | bytes accessed | tf_op | source)
XLA Modules:
  0.0 222.9 jit_solution(4828638175109133444)
XLA Ops:
  0.0 15.2 %all_gather.24 = bf16[1,128,320]{2,1,0:T(8,128)(2,1)S(1)} all-gather(bf16[1,32,320]{2,1,0:T(8,128)(2,1)} %param.10), channel_id=1, replica_groups=mesh['tiles'=2,'disp'=4,'rows'=2,'cols'=2] {'disp'}, dimensions={1}, use_global_device_ids=true | all-gather | bytes 102400 | tf_op jit(solution)/shard_map/all_gather | solution.py:117
  16.5 13.7 %all_gather.25 = bf16[1,128,320]{2,1,0:T(8,128)(2,1)S(1)} all-gather(bf16[1,32,320]{2,1,0:T(8,128)(2,1)} %param.9), channel_id=1, replica_groups=mesh['tiles'=2,'disp'=4,'rows'=2,'cols'=2] {'disp'}, dimensions={1}, use_global_device_ids=true | all-gather | bytes 102400 | tf_op jit(solution)/shard_map/all_gather | solution.py:116
  30.7 23.6 %while.31 = (s32[]{:T(128)}, bf16[16,40,1,128]{3,1,2,0:T(8,128)(2,1)S(1)}, s32[16]{0:T(128)S(1)}, s32[]{:T(128)}, bf16[1,384,320]{1,2,0:T(8,128)(2,1)S(1)}, /*in...) while((s32[]{:T(128)}, ...), condition=%wide.region_1.2_spmd, body=%wide.region_0.1_spmd.sunk | while | flops 174090 | bytes 215249 | solution.py:58
  54.4 3.3 %collective-permute-start.1 = (bf16[1,40,1,128]{3,1,0,2:T(8,128)(2,1)S(1)}, bf16[1,40,1,128]{3,1,0,2:T(8,128)(2,1)S(1)}, u32[]{:S(2)}, u32[]{:S(2)}) collective-permute-start(bf16[1,40,1,128]{3,1,0,2:T(8,128)(2,1)S(1)} %get-tuple-element.329), channel_id=1, source_target_pairs={{0,4},{4,8},{8,12},{1,5},{5,9},{9,13},{2,6},{6,10},{10,14},{3,7},{... | collective-permute-start | bytes 30728 | tf_op jit(solution)/shard_map/ppermute | solution.py:15
  59.1 4.2 %collective-permute-done.2 = bf16[1,40,1,128]{3,1,0,2:T(8,128)(2,1)S(1)} collective-permute-done((bf16[1,40,1,128]{3,1,0,2:T(8,128)(2,1)S(1)}, bf16[1,40,1,128]{3,1,0,2:T(8,128)(2,1)S(1)}, u32[]{:S(2)}, u32[]{:S(2)}) %collective-permute-start.2) | collective-permute-done | bytes 10272 | tf_op jit(solution)/shard_map/ppermute | solution.py:18
  63.3 3.4 %collective-permute-start.3 = (bf16[18,40,1,128]{3,1,0,2:T(8,128)(2,1)S(1)}, bf16[18,40,1,128]{3,1,0,2:T(8,128)(2,1)S(1)}, u32[]{:S(2)}, u32[]{:S(2)}) collective-permute-start(bf16[18,40,1,128]{3,1,0,2:T(8,128)(2,1)S(1)} %pad_maximum_fusion.48), channel_id=1, source_target_pairs={{0,2},{1,3},{4,6},{5,7},{8,10},{9,11},{12,14},{13,15},{16,18},{17,... | collective-permute-start | bytes 552968 | tf_op jit(solution)/shard_map/ppermute | solution.py:15
  68.0 1.7 collective-permute-done.3
  69.8 4.4 %collective-permute-done.4 = bf16[18,40,1,128]{3,1,0,2:T(8,128)(2,1)S(1)} collective-permute-done((bf16[18,40,1,128]{3,1,0,2:T(8,128)(2,1)S(1)}, bf16[18,40,1,128]{3,1,0,2:T(8,128)(2,1)S(1)}, u32[]{:S(2)}, u32[]{:S(2)}) %collective-permute-start.4) | collective-permute-done | bytes 184352 | tf_op jit(solution)/shard_map/ppermute | solution.py:18
  84.3 4.5 %collective-permute-start.7 = (f32[1,32,1,128]{3,1,0,2:T(8,128)S(1)}, f32[1,32,1,128]{3,1,0,2:T(8,128)S(1)}, u32[]{:S(2)}, u32[]{:S(2)}) collective-permute-start(f32[1,32,1,128]{3,1,0,2:T(8,128)S(1)} %get-tuple-element.324), channel_id=1, source_target_pairs={{0,4},{4,8},{8,12},{1,5},{5,9},{9,13},{2,6},{6,10},{10,14},{3,7},{... | collective-permute-start | bytes 49160 | tf_op jit(solution)/shard_map/ppermute | solution.py:15
  91.6 4.6 %collective-permute-start.9 = (f32[18,32,1,128]{3,1,0,2:T(8,128)S(1)}, f32[18,32,1,128]{3,1,0,2:T(8,128)S(1)}, u32[]{:S(2)}, u32[]{:S(2)}) collective-permute-start(f32[18,32,1,128]{3,1,0,2:T(8,128)S(1)} %pad_maximum_fusion.35), channel_id=1, source_target_pairs={{0,2},{1,3},{4,6},{5,7},{8,10},{9,11},{12,14},{13,15},{16,18},{17,... | collective-permute-start | bytes 884744 | tf_op jit(solution)/shard_map/ppermute | solution.py:15
  96.2 3.9 %collective-permute-done.10 = f32[18,32,1,128]{3,1,0,2:T(8,128)S(1)} collective-permute-done((f32[18,32,1,128]{3,1,0,2:T(8,128)S(1)}, f32[18,32,1,128]{3,1,0,2:T(8,128)S(1)}, u32[]{:S(2)}, u32[]{:S(2)}) %collective-permute-start.10) | collective-permute-done | bytes 294944 | tf_op jit(solution)/shard_map/ppermute | solution.py:18
  111.1 2.0 copy.100
  120.2 4.5 %collective-permute-start.13 = (f32[1,32,1,128]{3,1,0,2:T(8,128)S(1)}, f32[1,32,1,128]{3,1,0,2:T(8,128)S(1)}, u32[]{:S(2)}, u32[]{:S(2)}) collective-permute-start(f32[1,32,1,128]{3,1,0,2:T(8,128)S(1)} %get-tuple-element.322), channel_id=1, source_target_pairs={{0,4},{4,8},{8,12},{1,5},{5,9},{9,13},{2,6},{6,10},{10,14},{3,7},{... | collective-permute-start | bytes 49160 | tf_op jit(solution)/shard_map/ppermute | solution.py:15
  126.2 4.4 %collective-permute-start.15 = (f32[18,32,1,128]{3,1,0,2:T(8,128)S(1)}, f32[18,32,1,128]{3,1,0,2:T(8,128)S(1)}, u32[]{:S(2)}, u32[]{:S(2)}) collective-permute-start(f32[18,32,1,128]{3,1,0,2:T(8,128)S(1)} %pad_maximum_fusion.36), channel_id=1, source_target_pairs={{0,2},{1,3},{4,6},{5,7},{8,10},{9,11},{12,14},{13,15},{16,18},{17,... | collective-permute-start | bytes 884744 | tf_op jit(solution)/shard_map/ppermute | solution.py:15
  132.0 5.9 %collective-permute-done.15 = f32[18,32,1,128]{3,1,0,2:T(8,128)S(1)} collective-permute-done((f32[18,32,1,128]{3,1,0,2:T(8,128)S(1)}, f32[18,32,1,128]{3,1,0,2:T(8,128)S(1)}, u32[]{:S(2)}, u32[]{:S(2)}) %collective-permute-start.15) | collective-permute-done | bytes 294944 | tf_op jit(solution)/shard_map/ppermute | solution.py:15
  137.9 4.1 %collective-permute-done.16 = f32[18,32,1,128]{3,1,0,2:T(8,128)S(1)} collective-permute-done((f32[18,32,1,128]{3,1,0,2:T(8,128)S(1)}, f32[18,32,1,128]{3,1,0,2:T(8,128)S(1)}, u32[]{:S(2)}, u32[]{:S(2)}) %collective-permute-start.16) | collective-permute-done | bytes 294944 | tf_op jit(solution)/shard_map/ppermute | solution.py:18
  151.7 2.0 copy.111
  160.8 4.5 %collective-permute-start.19 = (f32[1,32,1,128]{3,1,0,2:T(8,128)S(1)}, f32[1,32,1,128]{3,1,0,2:T(8,128)S(1)}, u32[]{:S(2)}, u32[]{:S(2)}) collective-permute-start(f32[1,32,1,128]{3,1,0,2:T(8,128)S(1)} %get-tuple-element.320), channel_id=1, source_target_pairs={{0,4},{4,8},{8,12},{1,5},{5,9},{9,13},{2,6},{6,10},{10,14},{3,7},{... | collective-permute-start | bytes 49160 | tf_op jit(solution)/shard_map/ppermute | solution.py:15
  169.6 5.6 %collective-permute-done.21 = f32[18,32,1,128]{3,1,0,2:T(8,128)S(1)} collective-permute-done((f32[18,32,1,128]{3,1,0,2:T(8,128)S(1)}, f32[18,32,1,128]{3,1,0,2:T(8,128)S(1)}, u32[]{:S(2)}, u32[]{:S(2)}) %collective-permute-start.21) | collective-permute-done | bytes 294944 | tf_op jit(solution)/shard_map/ppermute | solution.py:15
  175.2 4.1 %collective-permute-done.22 = f32[18,32,1,128]{3,1,0,2:T(8,128)S(1)} collective-permute-done((f32[18,32,1,128]{3,1,0,2:T(8,128)S(1)}, f32[18,32,1,128]{3,1,0,2:T(8,128)S(1)}, u32[]{:S(2)}, u32[]{:S(2)}) %collective-permute-start.22) | collective-permute-done | bytes 294944 | tf_op jit(solution)/shard_map/ppermute | solution.py:18
  186.5 2.0 copy.122
  193.5 11.7 %all-gather.5 = f32[4,1,128]{2,1,0:T(1,128)S(1)} all-gather(f32[1,1,128]{2,1,0:T(1,128)S(1)} %bitcast.290), channel_id=4, replica_groups=mesh['tiles'=2,'disp'=4,'rows'=2,'cols'=2] {'disp'}, dimensions={0}, use_global_device_ids=true | all-gather | bytes 2560 | tf_op jit(solution)/shard_map/all_gather | solution.py:30
  205.1 7.5 %all-gather.4 = f32[4,1,128]{2,1,0:T(1,128)S(1)} all-gather(f32[1,1,128]{2,1,0:T(1,128)S(1)} %bitcast.289), channel_id=3, replica_groups=mesh['tiles'=2,'disp'=4,'rows'=2,'cols'=2] {'disp'}, dimensions={0}, use_global_device_ids=true | all-gather | bytes 2560 | tf_op jit(solution)/shard_map/all_gather | solution.py:30
  212.6 9.5 %all-gather.3 = f32[4,1,128]{2,1,0:T(1,128)S(1)} all-gather(f32[1,1,128]{2,1,0:T(1,128)S(1)} %bitcast.288), channel_id=2, replica_groups=mesh['tiles'=2,'disp'=4,'rows'=2,'cols'=2] {'disp'}, dimensions={0}, use_global_device_ids=true | all-gather | bytes 2560 | tf_op jit(solution)/shard_map/all_gather | solution.py:30
  (239 shorter events, 84.2 us)
Async XLA Ops:
  15.2 15.1 %collective-permute-start = (bf16[1,128,320]{2,1,0:T(8,128)(2,1)S(1)}, bf16[1,128,320]{2,1,0:T(8,128)(2,1)S(1)}, u32[]{:S(2)}, u32[]{:S(2)}) collective-permute-start(bf16[1,128,320]{2,1,0:T(8,128)(2,1)S(1)} %all_gather.24), channel_id=1, source_target_pairs={{0,1},{2,3},{4,5},{6,7},{8,9},{10,11},{12,13},{14,15},{16,17},{18,... | collective-permute-start | bytes 245768 | tf_op jit(solution)/shard_map/ppermute | solution.py:26
  54.4 4.7 %collective-permute-start.1 = (bf16[1,40,1,128]{3,1,0,2:T(8,128)(2,1)S(1)}, bf16[1,40,1,128]{3,1,0,2:T(8,128)(2,1)S(1)}, u32[]{:S(2)}, u32[]{:S(2)}) collective-permute-start(bf16[1,40,1,128]{3,1,0,2:T(8,128)(2,1)S(1)} %get-tuple-element.329), channel_id=1, source_target_pairs={{0,4},{4,8},{8,12},{1,5},{5,9},{9,13},{2,6},{6,10},{10,14},{3,7},{... | collective-permute-start | bytes 30728 | tf_op jit(solution)/shard_map/ppermute | solution.py:15
  57.7 5.6 %collective-permute-start.2 = (bf16[1,40,1,128]{3,1,0,2:T(8,128)(2,1)S(1)}, bf16[1,40,1,128]{3,1,0,2:T(8,128)(2,1)S(1)}, u32[]{:S(2)}, u32[]{:S(2)}) collective-permute-start(bf16[1,40,1,128]{3,1,0,2:T(8,128)(2,1)S(1)} %get-tuple-element.330), channel_id=1, source_target_pairs={{4,0},{8,4},{12,8},{5,1},{9,5},{13,9},{6,2},{10,6},{14,10},{7,3},{... | collective-permute-start | bytes 30728 | tf_op jit(solution)/shard_map/ppermute | solution.py:18
  63.3 6.4 %collective-permute-start.3 = (bf16[18,40,1,128]{3,1,0,2:T(8,128)(2,1)S(1)}, bf16[18,40,1,128]{3,1,0,2:T(8,128)(2,1)S(1)}, u32[]{:S(2)}, u32[]{:S(2)}) collective-permute-start(bf16[18,40,1,128]{3,1,0,2:T(8,128)(2,1)S(1)} %pad_maximum_fusion.48), channel_id=1, source_target_pairs={{0,2},{1,3},{4,6},{5,7},{8,10},{9,11},{12,14},{13,15},{16,18},{17,... | collective-permute-start | bytes 552968 | tf_op jit(solution)/shard_map/ppermute | solution.py:15
  66.7 7.4 %collective-permute-start.4 = (bf16[18,40,1,128]{3,1,0,2:T(8,128)(2,1)S(1)}, bf16[18,40,1,128]{3,1,0,2:T(8,128)(2,1)S(1)}, u32[]{:S(2)}, u32[]{:S(2)}) collective-permute-start(bf16[18,40,1,128]{3,1,0,2:T(8,128)(2,1)S(1)} %pad_maximum_fusion.48), channel_id=1, source_target_pairs={{2,0},{3,1},{6,4},{7,5},{10,8},{11,9},{14,12},{15,13},{18,16},{19,... | collective-permute-start | bytes 552968 | tf_op jit(solution)/shard_map/ppermute | solution.py:18
  75.0 3.7 %collective-permute-start.5 = (bf16[18,40,3,1]{1,0,3,2:T(8,128)(2,1)S(1)}, bf16[18,40,3,1]{1,0,3,2:T(8,128)(2,1)S(1)}, u32[]{:S(2)}, u32[]{:S(2)}) collective-permute-start(bf16[18,40,3,1]{1,0,3,2:T(8,128)(2,1)S(1)} %copy.89), channel_id=1, source_target_pairs={{0,1},{2,3},{4,5},{6,7},{8,9},{10,11},{12,13},{14,15},{16,17},{18,... | collective-permute-start | bytes 12968 | tf_op jit(solution)/shard_map/ppermute | solution.py:15
  83.0 5.9 %collective-permute-start.8 = (f32[1,32,1,128]{3,1,2,0:T(8,128)S(1)}, f32[1,32,1,128]{3,1,2,0:T(8,128)S(1)}, u32[]{:S(2)}, u32[]{:S(2)}) collective-permute-start(f32[1,32,1,128]{3,1,2,0:T(8,128)S(1)} %get-tuple-element.325), channel_id=1, source_target_pairs={{4,0},{8,4},{12,8},{5,1},{9,5},{13,9},{6,2},{10,6},{14,10},{7,3},{... | collective-permute-start | bytes 49160 | tf_op jit(solution)/shard_map/ppermute | solution.py:18
  84.3 6.0 %collective-permute-start.7 = (f32[1,32,1,128]{3,1,0,2:T(8,128)S(1)}, f32[1,32,1,128]{3,1,0,2:T(8,128)S(1)}, u32[]{:S(2)}, u32[]{:S(2)}) collective-permute-start(f32[1,32,1,128]{3,1,0,2:T(8,128)S(1)} %get-tuple-element.324), channel_id=1, source_target_pairs={{0,4},{4,8},{8,12},{1,5},{5,9},{9,13},{2,6},{6,10},{10,14},{3,7},{... | collective-permute-start | bytes 49160 | tf_op jit(solution)/shard_map/ppermute | solution.py:15
  90.3 9.8 %collective-permute-start.10 = (f32[18,32,1,128]{3,1,0,2:T(8,128)S(1)}, f32[18,32,1,128]{3,1,0,2:T(8,128)S(1)}, u32[]{:S(2)}, u32[]{:S(2)}) collective-permute-start(f32[18,32,1,128]{3,1,0,2:T(8,128)S(1)} %pad_maximum_fusion.35), channel_id=1, source_target_pairs={{2,0},{3,1},{6,4},{7,5},{10,8},{11,9},{14,12},{15,13},{18,16},{19,... | collective-permute-start | bytes 884744 | tf_op jit(solution)/shard_map/ppermute | solution.py:18
  91.6 9.7 %collective-permute-start.9 = (f32[18,32,1,128]{3,1,0,2:T(8,128)S(1)}, f32[18,32,1,128]{3,1,0,2:T(8,128)S(1)}, u32[]{:S(2)}, u32[]{:S(2)}) collective-permute-start(f32[18,32,1,128]{3,1,0,2:T(8,128)S(1)} %pad_maximum_fusion.35), channel_id=1, source_target_pairs={{0,2},{1,3},{4,6},{5,7},{8,10},{9,11},{12,14},{13,15},{16,18},{17,... | collective-permute-start | bytes 884744 | tf_op jit(solution)/shard_map/ppermute | solution.py:15
  102.2 6.5 %collective-permute-start.11 = (f32[18,32,3,1]{1,3,2,0:T(1,128)S(1)}, f32[18,32,3,1]{1,3,2,0:T(1,128)S(1)}, u32[]{:S(2)}, u32[]{:S(2)}) collective-permute-start(f32[18,32,3,1]{1,3,2,0:T(1,128)S(1)} %copy.97), channel_id=1, source_target_pairs={{0,1},{2,3},{4,5},{6,7},{8,9},{10,11},{12,13},{14,15},{16,17},{18,... | collective-permute-start | bytes 20744 | tf_op jit(solution)/shard_map/ppermute | solution.py:15
  107.3 3.8 %collective-permute-start.12 = (f32[18,32,3,1]{1,3,2,0:T(1,128)}, f32[18,32,3,1]{1,3,2,0:T(1,128)}, u32[]{:S(2)}, u32[]{:S(2)}) collective-permute-start(f32[18,32,3,1]{1,3,2,0:T(1,128)} %copy.99), channel_id=1, source_target_pairs={{1,0},{3,2},{5,4},{7,6},{9,8},{11,10},{13,12},{15,14},{17,16},{19,... | collective-permute-start | bytes 20744 | tf_op jit(solution)/shard_map/ppermute | solution.py:18
  118.9 5.9 %collective-permute-start.14 = (f32[1,32,1,128]{3,1,2,0:T(8,128)S(1)}, f32[1,32,1,128]{3,1,2,0:T(8,128)S(1)}, u32[]{:S(2)}, u32[]{:S(2)}) collective-permute-start(f32[1,32,1,128]{3,1,2,0:T(8,128)S(1)} %get-tuple-element.323), channel_id=1, source_target_pairs={{4,0},{8,4},{12,8},{5,1},{9,5},{13,9},{6,2},{10,6},{14,10},{7,3},{... | collective-permute-start | bytes 49160 | tf_op jit(solution)/shard_map/ppermute | solution.py:18
  120.2 6.0 %collective-permute-start.13 = (f32[1,32,1,128]{3,1,0,2:T(8,128)S(1)}, f32[1,32,1,128]{3,1,0,2:T(8,128)S(1)}, u32[]{:S(2)}, u32[]{:S(2)}) collective-permute-start(f32[1,32,1,128]{3,1,0,2:T(8,128)S(1)} %get-tuple-element.322), channel_id=1, source_target_pairs={{0,4},{4,8},{8,12},{1,5},{5,9},{9,13},{2,6},{6,10},{10,14},{3,7},{... | collective-permute-start | bytes 49160 | tf_op jit(solution)/shard_map/ppermute | solution.py:15
  126.2 11.7 %collective-permute-start.15 = (f32[18,32,1,128]{3,1,0,2:T(8,128)S(1)}, f32[18,32,1,128]{3,1,0,2:T(8,128)S(1)}, u32[]{:S(2)}, u32[]{:S(2)}) collective-permute-start(f32[18,32,1,128]{3,1,0,2:T(8,128)S(1)} %pad_maximum_fusion.36), channel_id=1, source_target_pairs={{0,2},{1,3},{4,6},{5,7},{8,10},{9,11},{12,14},{13,15},{16,18},{17,... | collective-permute-start | bytes 884744 | tf_op jit(solution)/shard_map/ppermute | solution.py:15
  130.7 11.4 %collective-permute-start.16 = (f32[18,32,1,128]{3,1,0,2:T(8,128)S(1)}, f32[18,32,1,128]{3,1,0,2:T(8,128)S(1)}, u32[]{:S(2)}, u32[]{:S(2)}) collective-permute-start(f32[18,32,1,128]{3,1,0,2:T(8,128)S(1)} %pad_maximum_fusion.36), channel_id=1, source_target_pairs={{2,0},{3,1},{6,4},{7,5},{10,8},{11,9},{14,12},{15,13},{18,16},{19,... | collective-permute-start | bytes 884744 | tf_op jit(solution)/shard_map/ppermute | solution.py:18
  142.8 6.4 %collective-permute-start.17 = (f32[18,32,3,1]{1,3,2,0:T(1,128)S(1)}, f32[18,32,3,1]{1,3,2,0:T(1,128)S(1)}, u32[]{:S(2)}, u32[]{:S(2)}) collective-permute-start(f32[18,32,3,1]{1,3,2,0:T(1,128)S(1)} %copy.108), channel_id=1, source_target_pairs={{0,1},{2,3},{4,5},{6,7},{8,9},{10,11},{12,13},{14,15},{16,17},{18,... | collective-permute-start | bytes 20744 | tf_op jit(solution)/shard_map/ppermute | solution.py:15
  147.7 3.9 %collective-permute-start.18 = (f32[18,32,3,1]{1,3,2,0:T(1,128)}, f32[18,32,3,1]{1,3,2,0:T(1,128)}, u32[]{:S(2)}, u32[]{:S(2)}) collective-permute-start(f32[18,32,3,1]{1,3,2,0:T(1,128)} %copy.110), channel_id=1, source_target_pairs={{1,0},{3,2},{5,4},{7,6},{9,8},{11,10},{13,12},{15,14},{17,16},{19,... | collective-permute-start | bytes 20744 | tf_op jit(solution)/shard_map/ppermute | solution.py:18
  159.5 5.9 %collective-permute-start.20 = (f32[1,32,1,128]{3,1,2,0:T(8,128)S(1)}, f32[1,32,1,128]{3,1,2,0:T(8,128)S(1)}, u32[]{:S(2)}, u32[]{:S(2)}) collective-permute-start(f32[1,32,1,128]{3,1,2,0:T(8,128)S(1)} %get-tuple-element.321), channel_id=1, source_target_pairs={{4,0},{8,4},{12,8},{5,1},{9,5},{13,9},{6,2},{10,6},{14,10},{7,3},{... | collective-permute-start | bytes 49160 | tf_op jit(solution)/shard_map/ppermute | solution.py:18
  160.8 6.0 %collective-permute-start.19 = (f32[1,32,1,128]{3,1,0,2:T(8,128)S(1)}, f32[1,32,1,128]{3,1,0,2:T(8,128)S(1)}, u32[]{:S(2)}, u32[]{:S(2)}) collective-permute-start(f32[1,32,1,128]{3,1,0,2:T(8,128)S(1)} %get-tuple-element.320), channel_id=1, source_target_pairs={{0,4},{4,8},{8,12},{1,5},{5,9},{9,13},{2,6},{6,10},{10,14},{3,7},{... | collective-permute-start | bytes 49160 | tf_op jit(solution)/shard_map/ppermute | solution.py:15
  166.8 8.4 %collective-permute-start.21 = (f32[18,32,1,128]{3,1,0,2:T(8,128)S(1)}, f32[18,32,1,128]{3,1,0,2:T(8,128)S(1)}, u32[]{:S(2)}, u32[]{:S(2)}) collective-permute-start(f32[18,32,1,128]{3,1,0,2:T(8,128)S(1)} %pad_maximum_fusion.37), channel_id=1, source_target_pairs={{0,2},{1,3},{4,6},{5,7},{8,10},{9,11},{12,14},{13,15},{16,18},{17,... | collective-permute-start | bytes 884744 | tf_op jit(solution)/shard_map/ppermute | solution.py:15
  168.3 11.1 %collective-permute-start.22 = (f32[18,32,1,128]{3,1,0,2:T(8,128)S(1)}, f32[18,32,1,128]{3,1,0,2:T(8,128)S(1)}, u32[]{:S(2)}, u32[]{:S(2)}) collective-permute-start(f32[18,32,1,128]{3,1,0,2:T(8,128)S(1)} %pad_maximum_fusion.37), channel_id=1, source_target_pairs={{2,0},{3,1},{6,4},{7,5},{10,8},{11,9},{14,12},{15,13},{18,16},{19,... | collective-permute-start | bytes 884744 | tf_op jit(solution)/shard_map/ppermute | solution.py:18
  180.1 3.9 %collective-permute-start.23 = (f32[18,32,3,1]{1,3,2,0:T(1,128)S(1)}, f32[18,32,3,1]{1,3,2,0:T(1,128)S(1)}, u32[]{:S(2)}, u32[]{:S(2)}) collective-permute-start(f32[18,32,3,1]{1,3,2,0:T(1,128)S(1)} %copy.119), channel_id=1, source_target_pairs={{0,1},{2,3},{4,5},{6,7},{8,9},{10,11},{12,13},{14,15},{16,17},{18,... | collective-permute-start | bytes 20744 | tf_op jit(solution)/shard_map/ppermute | solution.py:15
  182.7 3.8 %collective-permute-start.24 = (f32[18,32,3,1]{1,3,2,0:T(1,128)}, f32[18,32,3,1]{1,3,2,0:T(1,128)}, u32[]{:S(2)}, u32[]{:S(2)}) collective-permute-start(f32[18,32,3,1]{1,3,2,0:T(1,128)} %copy.121), channel_id=1, source_target_pairs={{1,0},{3,2},{5,4},{7,6},{9,8},{11,10},{13,12},{15,14},{17,16},{19,... | collective-permute-start | bytes 20744 | tf_op jit(solution)/shard_map/ppermute | solution.py:18
  (19 other events, 90.4 us)
where the time goes:
time: 224 us; the launch traced here: 223 us
  blocking collectives  57.6 us (26%)
  starting transfers between devices  53.4 us (24%)
  waiting for transfers between devices  40.8 us (18%)
  local copies, waits for them, and re-layouts  35.7 us (16%)
  other arithmetic  13.7 us (6%)
  loops' own time  10.9 us (5%)
  matrix products  9.94 us (4%)
    ppermute x12, starting transfers between devices, extended_2(): lax.ppermute(lax.slice_in_dim(block, block.shape[dim] - width, None, axis...  36.4 us
    all_gather x3, blocking collectives, combined_all(): gathered = jax.tree.map(lambda a: lax.all_gather(a, axis), part)  28.7 us
    ppermute x12, waiting for transfers between devices, extended_2(): lax.ppermute(lax.slice_in_dim(block, 0, width, axis=dim), axis, backward)  22 us
    ppermute x12, waiting for transfers between devices, extended_2(): lax.ppermute(lax.slice_in_dim(block, block.shape[dim] - width, None, axis...  18.8 us
    ppermute x12, starting transfers between devices, extended_2(): lax.ppermute(lax.slice_in_dim(block, 0, width, axis=dim), axis, backward)  15.6 us
    all_gather x1, blocking collectives, shards(): lax.all_gather(right_feat, 'disp', axis=1, tiled=True)  15.2 us
    all_gather x1, blocking collectives, shards(): lax.all_gather(left_feat, 'disp', axis=1, tiled=True)  13.7 us
    another operation x1, loops' own time, correlate(): return lax.map(single, jnp.arange(count, dtype=jnp.int32))  10.8 us
  transfers between devices with their start and end apart: 25, of which 14 were waited for; matrix products, arithmetic and copies ran while one was open for 8% of the time, Pallas kernels for 0%

commit v1 on v0

--- a/solution.py
+++ b/solution.py
@@ -1,6 +1,8 @@
 import jax
 import jax.numpy as jnp
 from jax import lax
+from jax.experimental import pallas as pl
+from jax.experimental.pallas import tpu as pltpu
 from jax.sharding import PartitionSpec as P
 
 MID = 2
@@ -105,7 +107,7 @@
     )
 
 
-def shards(left_feat, right_feat, conv_first, conv_mid, conv_last):
+def general(left_feat, right_feat, conv_first, conv_mid, conv_last):
     piece_width = left_feat.shape[1]
     groups = conv_first.shape[2]
     disp_count = lax.axis_size("disp")
@@ -138,6 +140,319 @@
     return lax.dynamic_slice_in_dim(whole_row, lax.axis_index("disp") * piece_width, piece_width, 1)
 
 
+BF, F32 = jnp.bfloat16, jnp.float32
+NT = (((1,), (1,)), ((), ()))
+
+
+def dot(a, b, dims=(((1,), (0,)), ((), ()))):
+    return lax.dot_general(a, b, dims, preferred_element_type=F32)
+
+
+def iota(shape, dim):
+    return lax.broadcasted_iota(jnp.int32, shape, dim)
+
+
+def prep_kernel(cf_ref, cm_ref, cl_ref, w1_ref, wm_ref, wl_ref, perm_ref):
+    own = lax.axis_index("rows")
+
+    def strip(tap_of, a, h_in, eye):
+        rows = []
+        for e in (1, 0, -1):
+            for h_out in (0, 1):
+                rows.append(tap_of(9 * a + 3 * (h_in - h_out + 1) + (e + 1)))
+        rows.append(jnp.zeros((64, rows[0].shape[1]), BF))
+        return dot(eye, jnp.concatenate(rows, axis=0), NT)
+
+    def placed(base, w_in):
+        shift = 64 * (w_in - 1)
+        lane = iota(base.shape, 1)
+        moved = base if shift == 0 else pltpu.roll(base, shift % 256, axis=1)
+        keep = (lane >= shift) & (lane < shift + 192)
+        return jnp.where(keep, moved, 0.0).astype(BF)
+
+    def eye_of(n):
+        return (iota((n, n), 0) == iota((n, n), 1)).astype(F32).astype(BF)
+
+    eye40, eye32 = eye_of(40), eye_of(32)
+    for a in range(3):
+        parts = [strip(lambda t: cf_ref[t], a, h_in, eye40) for h_in in (0, 1)]
+        main = jnp.concatenate([p[:32] for p in parts], axis=0)
+        rest = jnp.concatenate([p[32:] for p in parts], axis=0)
+        w1_ref[a, 464:496] = jnp.zeros((32, 256), BF)
+        for w_in in range(-1, 5):
+            row = {-1: 320, 4: 256}.get(w_in, 64 * w_in)
+            w1_ref[a, row : row + 64] = placed(main, w_in)
+            row = {-1: 496, 4: 448}.get(w_in, 384 + 16 * w_in)
+            w1_ref[a, row : row + 16] = placed(rest, w_in)
+    for layer in range(2):
+        for a in range(3):
+            main = jnp.concatenate(
+                [strip(lambda t: cm_ref[layer, t], a, h_in, eye32) for h_in in (0, 1)], axis=0
+            )
+            for w_in in range(-1, 5):
+                block = placed(main, w_in)
+                if w_in == 4:
+                    rows = (256, 384)
+                elif w_in == -1:
+                    rows = (320, 448)
+                else:
+                    rows = (64 * w_in, 512 + 64 * w_in)
+                for row in rows:
+                    wm_ref[layer, a, row : row + 64] = block
+    cl = cl_ref[...]
+    clt = dot(eye32, cl, NT).astype(BF)
+    for w_in in range(-1, 5):
+        for h_in in (0, 1):
+            lane = iota((27, 128), 1)
+            a, e = lane // 4, w_in - lane % 4
+            b = h_in - own
+            tap = 9 * a + 3 * (b + 1) + (e + 1)
+            ok = (a < 3) & (e >= -1) & (e <= 1) & (b >= -1) & (b <= 1)
+            pick = (ok & (iota((27, 128), 0) == tap)).astype(F32).astype(BF)
+            block = dot(clt, pick).astype(BF)
+            if w_in == 4:
+                rows = (256, 384)
+            elif w_in == -1:
+                rows = (320, 448)
+            else:
+                rows = (64 * w_in, 512 + 64 * w_in)
+            for row in rows:
+                wl_ref[row + 32 * h_in : row + 32 * h_in + 32] = block
+    lane = iota((1, 1024), 1)
+    src = ((lane // 32) % 2) * 384 + (lane % 32) * 8 + lane // 128
+    perm_ref[:, :1024] = (iota((768, 1024), 0) == src).astype(F32).astype(BF)
+    lane = iota((1, 512), 1)
+    src = ((lane // 8) % 2) * 384 + (32 + lane % 8) * 8 + (lane // 128) * 2 + (lane // 64) % 2
+    perm_ref[:, 1024:] = (iota((768, 512), 0) == src).astype(F32).astype(BF)
+
+
+def prep(cf, cm, cl):
+    vm = pl.BlockSpec(memory_space=pltpu.VMEM)
+    return pl.pallas_call(
+        prep_kernel,
+        out_shape=(
+            jax.ShapeDtypeStruct((3, 512, 256), BF),
+            jax.ShapeDtypeStruct((2, 3, 768, 256), BF),
+            jax.ShapeDtypeStruct((768, 128), BF),
+            jax.ShapeDtypeStruct((768, 1536), BF),
+        ),
+        in_specs=[vm] * 3,
+        out_specs=[vm] * 4,
+        compiler_params=pltpu.CompilerParams(vmem_limit_bytes=40 * 2**20),
+        name="prep",
+    )(cf, cm, cl)
+
+
+def main_body(load_r, load_l, w1_ref, wm_ref, wl_ref, perm_ref, out_ref, win, rs, lp, xb1, xb, ys):
+    z = lax.axis_index("disp")
+    core = lax.axis_index("cols")
+    piece = core * 4 + z
+    win[...] = jnp.zeros_like(win)
+
+    def put(row, pair):
+        for h in (0, 1):
+            win[row : row + pair[h].shape[0], 384 * h : 384 * h + 320] = pair[h]
+
+    put(0, load_r(1, 0, 16))
+    put(16, load_r(-3, 16, 32))
+    put(32, load_r(-2, 0, 32))
+    put(64, load_r(-1, 0, 32))
+    put(96, load_r(0, 0, 32))
+    put(128, load_l(-1, 16, 32))
+    put(144, load_l(0, 0, 32))
+    put(176, load_l(1, 0, 16))
+    zp = dot(win[...], perm_ref[...])
+    for tile in range(12):
+        lp[tile] = zp[128:, 128 * tile : 128 * tile + 128]
+    zpr = zp[:128]
+    lane = iota((128, 1024), 1)
+    zm = jnp.concatenate(
+        [jnp.where((lane // 64) % 2 == ww, zpr[:, :1024], 0.0).astype(BF) for ww in (0, 1)], axis=0
+    )
+    lane = iota((128, 512), 1)
+    ze = jnp.concatenate(
+        [jnp.where((lane // 16) % 4 == ww, zpr[:, 1024:], 0.0).astype(BF) for ww in range(4)], axis=0
+    )
+    s, q = iota((112, 512), 0), iota((112, 512), 1)
+    r = q % 128
+    rel = jnp.where(r < 16, 32 + r, r - 96)
+    pick = (s == 40 + q // 128 - rel).astype(F32).astype(BF)
+    rsm = dot(pick[:, :256], zm)
+    rse = dot(pick, ze)
+    for tile in range(8):
+        rs[tile] = rsm[:, 128 * tile : 128 * tile + 128]
+    for tile in range(4):
+        rs[8 + tile] = rse[:, 128 * tile : 128 * tile + 128]
+
+    lane1 = iota((1, 128), 1)
+    low = lane1 < 64
+    zero64 = jnp.zeros((64, 64), BF)
+    xb1[0:64, 320:384] = zero64
+    xb1[576:640, 256:320] = zero64
+    kept = jnp.zeros((64, 128), BF)
+    for wb in range(10):
+        rows = slice(64 * wb, 64 * wb + 64)
+        r0 = 12 + 4 * wb
+        tiles = []
+        for half in range(2):
+            acc = None
+            start = 44 - 4 * wb - 2 * half
+            for c in range(8):
+                left = jnp.where(
+                    low,
+                    lp[c, r0 + 2 * half : r0 + 2 * half + 1],
+                    lp[c, r0 + 2 * half + 1 : r0 + 2 * half + 2],
+                )
+                term = left * rs[c, start : start + 64]
+                acc = term if acc is None else acc + term
+            tiles.append((acc * 0.125).astype(BF))
+        acc = None
+        start = 44 - 4 * wb
+        group = (lane1 // 16) % 4
+        for c in range(4):
+            left = lp[8 + c, r0 : r0 + 1]
+            for ww in (1, 2, 3):
+                left = jnp.where(group == ww, lp[8 + c, r0 + ww : r0 + ww + 1], left)
+            term = left * rs[8 + c, start : start + 64]
+            acc = term if acc is None else acc + term
+        rest = ((acc + pltpu.roll(acc, 64, axis=1)) * 0.125).astype(BF)
+        xb1[rows, 0:128] = tiles[0]
+        xb1[rows, 128:256] = tiles[1]
+        xb1[rows, 384:512] = rest
+        if wb > 0:
+            before = slice(64 * wb - 64, 64 * wb)
+            xb1[before, 256:320] = tiles[0][:, :64]
+            xb1[before, 448:464] = rest[:, 64:80]
+        xb1[rows, 496:512] = kept[:, 112:]
+        if wb < 9:
+            xb1[64 * wb + 64 : 64 * wb + 128, 320:384] = tiles[1][:, 64:]
+        kept = rest
+    xb1[576:640, 448:464] = jnp.zeros((64, 16), BF)
+
+    first_ok = piece > 0
+    last_ok = piece < 4 * lax.axis_size("cols") - 1
+    ys[...] = jnp.zeros_like(ys)
+
+    def layer(x, weights):
+        ym = dot(x, weights(0))
+        yc = dot(x, weights(1))
+        yp = dot(x, weights(2))
+        for tile in range(2):
+            for wb in range(10):
+                ys[tile, 0, wb, 8:72] = ym[64 * wb : 64 * wb + 64, 128 * tile : 128 * tile + 128]
+                ys[tile, 1, wb, 8:72] = yp[64 * wb : 64 * wb + 64, 128 * tile : 128 * tile + 128]
+        for wb in range(10):
+            halves = []
+            for tile in range(2):
+                total = (
+                    yc[64 * wb : 64 * wb + 64, 128 * tile : 128 * tile + 128]
+                    + ys[tile, 0, wb, 7:71]
+                    + ys[tile, 1, wb, 9:73]
+                )
+                total = jnp.maximum(total, 0.0)
+                if wb == 0:
+                    total = jnp.where(first_ok, total, 0.0)
+                if wb == 9:
+                    total = jnp.where(last_ok, total, 0.0)
+                halves.append(total)
+            rows = slice(64 * wb, 64 * wb + 64)
+            for tile in range(2):
+                hi = halves[tile].astype(BF)
+                lo = (halves[tile] - hi.astype(F32)).astype(BF)
+                for value, main, halo in ((hi, 0, 256), (lo, 512, 384)):
+                    xb[rows, main + 128 * tile : main + 128 * tile + 128] = value
+                    if tile == 0 and wb > 0:
+                        xb[64 * wb - 64 : 64 * wb, halo : halo + 64] = value[:, :64]
+                    if tile == 1 and wb < 9:
+                        xb[64 * wb + 64 : 64 * wb + 128, halo + 64 : halo + 128] = value[:, 64:]
+
+    for halo in (256, 384):
+        xb[0:64, halo + 64 : halo + 128] = zero64
+        xb[576:640, halo : halo + 64] = zero64
+    layer(xb1[...], lambda a: w1_ref[a])
+    layer(xb[...], lambda a: wm_ref[0, a])
+    layer(xb[...], lambda a: wm_ref[1, a])
+    y = dot(xb[64:576], wl_ref[...])
+    for wb in range(8):
+        ys[0, 0, wb, 8:72] = y[64 * wb : 64 * wb + 64]
+    cost = jnp.zeros((64, 128), F32)
+    for wb in range(8):
+        part = None
+        for a in range(3):
+            term = ys[0, 0, wb, 7 + a : 71 + a]
+            by = (4 * wb - 4 * a) % 128
+            term = term if by == 0 else pltpu.roll(term, by, axis=1)
+            part = term if part is None else part + term
+        cost = jnp.where(lane1 // 4 == wb, part, cost)
+    top = jnp.max(cost, axis=0, keepdims=True)
+    weight = jnp.exp(cost - top)
+    level = iota((64, 128), 0).astype(F32) * (1.0 / 64)
+    est = jnp.sum(weight * level, axis=0, keepdims=True) / jnp.sum(weight, axis=0, keepdims=True)
+    out_ref[...] = est[:, :32]
+
+
+SCRATCH = [
+    pltpu.VMEM((192, 768), BF),
+    pltpu.VMEM((12, 112, 128), F32),
+    pltpu.VMEM((12, 64, 128), F32),
+    pltpu.VMEM((640, 512), BF),
+    pltpu.VMEM((640, 768), BF),
+    pltpu.VMEM((2, 2, 10, 80, 128), F32),
+]
+
+
+def main_kernel(*refs):
+    g = refs[:8]
+    w1, wm, wl, perm, out, win, rs, lp, xb1, xb, ys, stack = refs[8:]
+    z, x, core = (lax.axis_index(n) for n in ("disp", "rows", "cols"))
+    piece = core * 4 + z
+    for i in range(8):
+        stack[i] = g[i][...]
+
+    def load(dp, base, lo, hi):
+        want = piece + dp
+        ok = (want >= 0) & (want < 8)
+        want = jnp.clip(want, 0, 7)
+        slot = 2 * (z ^ (want % 4)) + (core ^ (want // 4))
+        return [
+            jnp.where(ok, stack[slot, h ^ x, base + lo : base + hi], jnp.zeros((), BF)) for h in (0, 1)
+        ]
+
+    main_body(
+        lambda dp, lo, hi: load(dp, 0, lo, hi),
+        lambda dp, lo, hi: load(dp, 32, lo, hi),
+        w1, wm, wl, perm, out, win, rs, lp, xb1, xb, ys,
+    )
+
+
+def fast(left_feat, right_feat, conv_first, conv_mid, conv_last):
+    s = jnp.concatenate([right_feat, left_feat], axis=1)
+    swap = [(0, 1), (1, 0)]
+    s = jnp.concatenate([s, lax.ppermute(s, "rows", swap)], axis=0)
+    a = [s] + [lax.ppermute(s, "disp", [(i, i ^ k) for i in range(4)]) for k in (1, 2, 3)]
+    g = []
+    for t in a:
+        g += [t, lax.ppermute(t, "cols", swap)]
+    ws = prep(conv_first, conv_mid, conv_last.reshape(27, 32))
+    vm = pl.BlockSpec(memory_space=pltpu.VMEM)
+    return pl.pallas_call(
+        main_kernel,
+        out_shape=jax.ShapeDtypeStruct((1, 32), F32),
+        in_specs=[vm] * 12,
+        out_specs=vm,
+        scratch_shapes=SCRATCH + [pltpu.VMEM((8, 2, 64, 320), BF)],
+        compiler_params=pltpu.CompilerParams(vmem_limit_bytes=48 * 2**20),
+        name="cost_volume",
+    )(*g, *ws)
+
+
+def shards(left_feat, right_feat, conv_first, conv_mid, conv_last):
+    sizes = tuple(lax.axis_size(name) for name in ("disp", "rows", "cols"))
+    if sizes == (4, 2, 2) and left_feat.shape == (1, 32, 320) and conv_first.shape == (27, 32, 40):
+        return fast(left_feat, right_feat, conv_first, conv_mid, conv_last)
+    return general(left_feat, right_feat, conv_first, conv_mid, conv_last)
+
+
 def solution(mesh):
     return jax.shard_map(
         shards,

time: 224 us -> 32 us (0.14)
  blocking collectives: 57.6 us -> 0 us
  starting transfers between devices: 53.4 us -> 8.3 us
  waiting for transfers between devices: 40.8 us -> 8.63 us
  local copies, waits for them, and re-layouts: 35.7 us -> 5.55 us
  other arithmetic: 13.7 us -> 0.02 us
  loops' own time: 10.9 us -> 0 us
  matrix products: 9.94 us -> 0 us
  Pallas kernels: 0 us -> 9.12 us
    all_gather x5 -> x0, blocking collectives: 57.6 us -> none  [the longest x3 28.7 us: combined_all(): gathered = jax.tree.map(lambda a: lax.all_gather(a, axis), part)]
    ppermute x25 -> x8, starting transfers between devices: 53.4 us -> 8.3 us  [the longest x3 4.84 us: fast(): lax.ppermute(s, 'disp', [(i, i ^ k) for i in range(4)])]
    ppermute x25 -> x8, waiting for transfers between devices: 40.8 us -> 8.63 us  [the longest x3 6.56 us: fast(): lax.ppermute(s, 'disp', [(i, i ^ k) for i in range(4)])]
    dynamic_slice x17 -> x0, local copies, waits for them, and re-layouts: 11 us -> none  [the longest x16 10.4 us: correlate(): return lax.map(single, jnp.arange(count, dtype=jnp.int32))]
    ppermute x8 -> x0, local copies, waits for them, and re-layouts: 11 us -> none  [the longest x4 6.55 us: extended_2(): lax.ppermute(lax.slice_in_dim(block, 0, width, axis=dim), axis, backward)]
    another operation x2 -> x0, loops' own time: 10.9 us -> none  [the longest x1 10.8 us: correlate(): return lax.map(single, jnp.arange(count, dtype=jnp.int32))]
    dot_general x12 -> x0, matrix products: 9.94 us -> none  [convolve(): jnp.einsum('ok,dkn->don', taps, flat[disp_tap:disp_tap + depth_out], pref...]
    unnamed x24 -> x0, other arithmetic: 9.72 us -> none
  transfers between devices with their start and end apart: 25 -> 8, of which waited for: 14 -> 3; matrix products, arithmetic and copies ran while one was open for 8% -> 0% of each run, Pallas kernels for 0% -> 6%
where the time goes in v1:
time: 32 us; the launch traced here: 31.7 us
  Pallas kernels  9.12 us (28%)
  waiting for transfers between devices  8.63 us (27%)
  starting transfers between devices  8.3 us (26%)
  local copies, waits for them, and re-layouts  5.55 us (17%)
    pallas_call x1, Pallas kernels, fast(): pl.pallas_call(main_kernel, out_shape=jax.ShapeDtypeStruct((1, 32), F32),...  7.3 us
    ppermute x3, waiting for transfers between devices, fast(): lax.ppermute(s, 'disp', [(i, i ^ k) for i in range(4)])  6.56 us
    ppermute x3, starting transfers between devices, fast(): lax.ppermute(s, 'disp', [(i, i ^ k) for i in range(4)])  4.84 us
    unnamed x9, local copies, waits for them, and re-layouts  4.8 us
    ppermute x1, starting transfers between devices, fast(): s = jnp.concatenate([s, lax.ppermute(s, 'rows', swap)], axis=0)  2.94 us
    ppermute x1, waiting for transfers between devices, fast(): s = jnp.concatenate([s, lax.ppermute(s, 'rows', swap)], axis=0)  2.07 us
    pallas_call x1, Pallas kernels, prep(): pl.pallas_call(prep_kernel, out_shape=(jax.ShapeDtypeStruct((3, 512, 256)...  1.82 us
    concatenate x1, local copies, waits for them, and re-layouts, fast(): s = jnp.concatenate([right_feat, left_feat], axis=1)  0.75 us
  transfers between devices with their start and end apart: 8, of which 3 were waited for; matrix products, arithmetic and copies ran while one was open for 0% of the time, Pallas kernels for 6%

profile of v1, /device:TPU:0, one launch (start us, length us, event | category | flops | bytes accessed | tf_op | source)
XLA Modules:
  0.0 31.7 jit_solution(14728418383286002471)
XLA Ops:
  0.0 0.7 %constant_dynamic-update-slice_fusion.1 = bf16[1,64,320]{2,1,0:T(8,128)(2,1)S(1)} fusion(bf16[1,32,320]{2,1,0:T(8,128)(2,1)} %param.6), kind=kLoop, calls=%fused_computation.2 | loop fusion | bytes 45056
  0.7 0.7 %constant_dynamic-update-slice_fusion = bf16[1,64,320]{2,1,0:T(8,128)(2,1)S(1)} fusion(bf16[1,64,320]{2,1,0:T(8,128)(2,1)S(1)} %constant_dynamic-update-slice_fusion.1, bf16[1,32,320]{2,1,0:T(8,128)(2,1)} %param.5), kind=kLoop, calls=%fused_computation.1 | loop fusion | bytes 45056 | tf_op jit(solution)/shard_map/concatenate | solution.py:429
  1.5 2.9 %collective-permute-start = (bf16[1,64,320]{2,1,0:T(8,128)(2,1)S(1)}, bf16[1,64,320]{2,1,0:T(8,128)(2,1)S(1)}, u32[]{:S(2)}, u32[]{:S(2)}) collective-permute-start(bf16[1,64,320]{2,1,0:T(8,128)(2,1)S(1)} %constant_dynamic-update-slice_fusion), channel_id=1, source_target_pairs={{0,2},{2,0},{1,3},{3,1},{4,6},{6,4},{5,7},{7,5},{8,10},{10,8},{9,1... | collective-permute-start | bytes 122888 | tf_op jit(solution)/shard_map/ppermute | solution.py:431
  4.4 2.1 %collective-permute-done = bf16[1,64,320]{2,1,0:T(8,128)(2,1)S(1)} collective-permute-done((bf16[1,64,320]{2,1,0:T(8,128)(2,1)S(1)}, bf16[1,64,320]{2,1,0:T(8,128)(2,1)S(1)}, u32[]{:S(2)}, u32[]{:S(2)}) %collective-permute-start) | collective-permute-done | bytes 40992 | tf_op jit(solution)/shard_map/ppermute | solution.py:431
  6.5 4.2 %collective-permute-start.6 = (bf16[2,64,320]{2,1,0:T(8,128)(2,1)S(1)}, bf16[2,64,320]{2,1,0:T(8,128)(2,1)S(1)}, u32[]{:S(2)}, u32[]{:S(2)}) collective-permute-start(bf16[2,64,320]{2,1,0:T(8,128)(2,1)S(1)} %pad_maximum_fusion.refs_0_), channel_id=1, source_target_pairs={{0,12},{4,8},{8,4},{12,0},{1,13},{5,9},{9,5},{13,1},{2,14},{6,10},... | collective-permute-start | bytes 245768 | tf_op jit(solution)/shard_map/ppermute | solution.py:432
  10.7 0.0 collective-permute-start.4
  10.7 0.6 %collective-permute-start.2 = (bf16[2,64,320]{2,1,0:T(8,128)(2,1)S(1)}, bf16[2,64,320]{2,1,0:T(8,128)(2,1)S(1)}, u32[]{:S(2)}, u32[]{:S(2)}) collective-permute-start(bf16[2,64,320]{2,1,0:T(8,128)(2,1)S(1)} %pad_maximum_fusion.refs_0_), channel_id=1, source_target_pairs={{0,4},{4,0},{8,12},{12,8},{1,5},{5,1},{9,13},{13,9},{2,6},{6,2},{1... | collective-permute-start | bytes 245768 | tf_op jit(solution)/shard_map/ppermute | solution.py:432
  11.4 0.0 collective-permute-start.1
  11.4 2.5 %collective-permute-done.6.refs_6_ = bf16[2,64,320]{2,1,0:T(8,128)(2,1)S(1)} collective-permute-done((bf16[2,64,320]{2,1,0:T(8,128)(2,1)S(1)}, bf16[2,64,320]{2,1,0:T(8,128)(2,1)S(1)}, u32[]{:S(2)}, u32[]{:S(2)}) %collective-permute-start.6) | collective-permute-done | bytes 81952 | tf_op jit(solution)/shard_map/ppermute | solution.py:432
  13.8 0.0 collective-permute-start.7
  13.8 4.1 %collective-permute-done.4.refs_4_ = bf16[2,64,320]{2,1,0:T(8,128)(2,1)S(1)} collective-permute-done((bf16[2,64,320]{2,1,0:T(8,128)(2,1)S(1)}, bf16[2,64,320]{2,1,0:T(8,128)(2,1)S(1)}, u32[]{:S(2)}, u32[]{:S(2)}) %collective-permute-start.4) | collective-permute-done | bytes 81952 | tf_op jit(solution)/shard_map/ppermute | solution.py:432
  17.9 0.0 collective-permute-start.5
  17.9 0.0 collective-permute-done.2.refs_2_
  17.9 0.5 %collective-permute-start.3 = (bf16[2,64,320]{2,1,0:T(8,128)(2,1)S(1)}, bf16[2,64,320]{2,1,0:T(8,128)(2,1)S(1)}, u32[]{:S(2)}, u32[]{:S(2)}) collective-permute-start(bf16[2,64,320]{2,1,0:T(8,128)(2,1)S(1)} %collective-permute-done.2.refs_2_), channel_id=1, source_target_pairs={{0,1},{1,0},{2,3},{3,2},{4,5},{5,4},{6,7},{7,6},{8,9},{9,8},{10,11... | collective-permute-start | bytes 245768 | tf_op jit(solution)/shard_map/ppermute | solution.py:435
  18.4 1.0 %copy-done.1 = bf16[2,27,32,32]{3,2,1,0:T(8,128)(2,1)S(1)} copy-done((bf16[2,27,32,32]{3,2,1,0:T(8,128)(2,1)S(1)}, bf16[2,27,32,32]{3,2,1,0:T(8,128)(2,1)}, u32[]{:S(2)}) %copy-start.1) | copy-done | bytes 110616
  19.5 0.9 %copy-done.2 = bf16[27,32,40]{2,1,0:T(8,128)(2,1)S(1)} copy-done((bf16[27,32,40]{2,1,0:T(8,128)(2,1)S(1)}, bf16[27,32,40]{2,1,0:T(8,128)(2,1)}, u32[]{:S(2)}) %copy-start.2) | copy-done | bytes 69144
  20.4 0.7 %copy-done.3 = bf16[27,1,32]{2,0,1:T(8,128)(2,1)S(1)} copy-done((bf16[27,1,32]{2,0,1:T(8,128)(2,1)S(1)}, bf16[27,1,32]{2,0,1:T(8,128)(2,1)}, u32[]{:S(2)}) %copy-start.3) | copy-done | bytes 1752
  21.1 1.8 %prep.1 = (bf16[3,512,256]{2,1,0:T(8,128)(2,1)S(1)}, bf16[2,3,768,256]{3,2,1,0:T(8,128)(2,1)S(1)}, bf16[768,128]{1,0:T(8,128)(2,1)S(1)}, bf16[768,1536]{1,0:T(8,128)(2,1)S(1)}) custom-call(bf16[27,32,40]{2,1,0:T(8,128)(2,1)S(1)} %copy-done.2, bf16[2,27,32,32]{3,2,1,0:T(8,128)(2,1)S(1)} %copy-done.1, bf16[27,32]{1,0:T(8,128)(2,1)S(1)} %bitcast.1), custom_call_target="tpu_custom_call" | custom-call | tf_op jit(solution)/shard_map/prep/pallas_call | solution.py:231
  22.9 1.4 %copy-done = bf16[768,1536]{1,0:T(8,128)(2,1)} copy-done((bf16[768,1536]{1,0:T(8,128)(2,1)}, bf16[768,1536]{1,0:T(8,128)(2,1)S(1)}, u32[]{:S(2)}) %copy-start) | copy-done | bytes 2359320
  24.3 0.0 collective-permute-done.1.refs_1_
  24.3 0.0 collective-permute-done.7.refs_7_
  24.3 0.0 collective-permute-done.5.refs_5_
  24.4 0.0 collective-permute-done.3.refs_3_
  24.4 7.3 %cost_volume.1 = f32[1,32]{1,0:T(1,128)} custom-call(bf16[2,64,320]{2,1,0:T(8,128)(2,1)S(1)} %pad_maximum_fusion.refs_0_, bf16[2,64,320]{2,1,0:T(8,128)(2,1)S(1)} %collective-permute-done.1.refs_1_, bf16[2,64,320]{2,1,0:T(8,128)(2,1)S(1)} %collective-permute-done.2.refs_2_, bf16[2,64,320]{2,1,0:T(8,128)(2,1)S(1)} %collective-permute-done.3.refs_3_, ...), custom_call_target="tpu_custom_call" | custom-call | tf_op jit(solution)/shard_map/cost_volume/pallas_call | solution.py:438
  (5 shorter events, 0.0 us)
Async XLA Ops:
  1.5 5.0 %collective-permute-start = (bf16[1,64,320]{2,1,0:T(8,128)(2,1)S(1)}, bf16[1,64,320]{2,1,0:T(8,128)(2,1)S(1)}, u32[]{:S(2)}, u32[]{:S(2)}) collective-permute-start(bf16[1,64,320]{2,1,0:T(8,128)(2,1)S(1)} %constant_dynamic-update-slice_fusion), channel_id=1, source_target_pairs={{0,2},{2,0},{1,3},{3,1},{4,6},{6,4},{5,7},{7,5},{8,10},{10,8},{9,1... | collective-permute-start | bytes 122888 | tf_op jit(solution)/shard_map/ppermute | solution.py:431
  6.5 7.3 %collective-permute-start.6 = (bf16[2,64,320]{2,1,0:T(8,128)(2,1)S(1)}, bf16[2,64,320]{2,1,0:T(8,128)(2,1)S(1)}, u32[]{:S(2)}, u32[]{:S(2)}) collective-permute-start(bf16[2,64,320]{2,1,0:T(8,128)(2,1)S(1)} %pad_maximum_fusion.refs_0_), channel_id=1, source_target_pairs={{0,12},{4,8},{8,4},{12,0},{1,13},{5,9},{9,5},{13,1},{2,14},{6,10},... | collective-permute-start | bytes 245768 | tf_op jit(solution)/shard_map/ppermute | solution.py:432
  10.7 7.2 %collective-permute-start.4 = (bf16[2,64,320]{2,1,0:T(8,128)(2,1)S(1)}, bf16[2,64,320]{2,1,0:T(8,128)(2,1)S(1)}, u32[]{:S(2)}, u32[]{:S(2)}) collective-permute-start(bf16[2,64,320]{2,1,0:T(8,128)(2,1)S(1)} %pad_maximum_fusion.refs_0_), channel_id=1, source_target_pairs={{0,8},{4,12},{8,0},{12,4},{1,9},{5,13},{9,1},{13,5},{2,10},{6,14},... | collective-permute-start | bytes 245768 | tf_op jit(solution)/shard_map/ppermute | solution.py:432
  10.7 7.2 %collective-permute-start.2 = (bf16[2,64,320]{2,1,0:T(8,128)(2,1)S(1)}, bf16[2,64,320]{2,1,0:T(8,128)(2,1)S(1)}, u32[]{:S(2)}, u32[]{:S(2)}) collective-permute-start(bf16[2,64,320]{2,1,0:T(8,128)(2,1)S(1)} %pad_maximum_fusion.refs_0_), channel_id=1, source_target_pairs={{0,4},{4,0},{8,12},{12,8},{1,5},{5,1},{9,13},{13,9},{2,6},{6,2},{1... | collective-permute-start | bytes 245768 | tf_op jit(solution)/shard_map/ppermute | solution.py:432
  11.4 13.0 %collective-permute-start.1 = (bf16[2,64,320]{2,1,0:T(8,128)(2,1)S(1)}, bf16[2,64,320]{2,1,0:T(8,128)(2,1)S(1)}, u32[]{:S(2)}, u32[]{:S(2)}) collective-permute-start(bf16[2,64,320]{2,1,0:T(8,128)(2,1)S(1)} %pad_maximum_fusion.refs_0_), channel_id=1, source_target_pairs={{0,1},{1,0},{2,3},{3,2},{4,5},{5,4},{6,7},{7,6},{8,9},{9,8},{10,11... | collective-permute-start | bytes 245768 | tf_op jit(solution)/shard_map/ppermute | solution.py:435
  13.8 10.5 %collective-permute-start.7 = (bf16[2,64,320]{2,1,0:T(8,128)(2,1)S(1)}, bf16[2,64,320]{2,1,0:T(8,128)(2,1)S(1)}, u32[]{:S(2)}, u32[]{:S(2)}) collective-permute-start(bf16[2,64,320]{2,1,0:T(8,128)(2,1)S(1)} %collective-permute-done.6.refs_6_), channel_id=1, source_target_pairs={{0,1},{1,0},{2,3},{3,2},{4,5},{5,4},{6,7},{7,6},{8,9},{9,8},{10,11... | collective-permute-start | bytes 245768 | tf_op jit(solution)/shard_map/ppermute | solution.py:435
  17.9 6.4 %collective-permute-start.5 = (bf16[2,64,320]{2,1,0:T(8,128)(2,1)S(1)}, bf16[2,64,320]{2,1,0:T(8,128)(2,1)S(1)}, u32[]{:S(2)}, u32[]{:S(2)}) collective-permute-start(bf16[2,64,320]{2,1,0:T(8,128)(2,1)S(1)} %collective-permute-done.4.refs_4_), channel_id=1, source_target_pairs={{0,1},{1,0},{2,3},{3,2},{4,5},{5,4},{6,7},{7,6},{8,9},{9,8},{10,11... | collective-permute-start | bytes 245768 | tf_op jit(solution)/shard_map/ppermute | solution.py:435
  17.9 6.4 %collective-permute-start.3 = (bf16[2,64,320]{2,1,0:T(8,128)(2,1)S(1)}, bf16[2,64,320]{2,1,0:T(8,128)(2,1)S(1)}, u32[]{:S(2)}, u32[]{:S(2)}) collective-permute-start(bf16[2,64,320]{2,1,0:T(8,128)(2,1)S(1)} %collective-permute-done.2.refs_2_), channel_id=1, source_target_pairs={{0,1},{1,0},{2,3},{3,2},{4,5},{5,4},{6,7},{7,6},{8,9},{9,8},{10,11... | collective-permute-start | bytes 245768 | tf_op jit(solution)/shard_map/ppermute | solution.py:435
  18.4 1.0 %copy-start.1 = (bf16[2,27,32,32]{3,2,1,0:T(8,128)(2,1)S(1)}, bf16[2,27,32,32]{3,2,1,0:T(8,128)(2,1)}, u32[]{:S(2)}) copy-start(bf16[2,27,32,32]{3,2,1,0:T(8,128)(2,1)} %cm_ref.1) | copy-start | bytes 331780
  19.5 0.9 %copy-start.2 = (bf16[27,32,40]{2,1,0:T(8,128)(2,1)S(1)}, bf16[27,32,40]{2,1,0:T(8,128)(2,1)}, u32[]{:S(2)}) copy-start(bf16[27,32,40]{2,1,0:T(8,128)(2,1)} %cf_ref.1) | copy-start | bytes 207364
  20.4 0.7 %copy-start.3 = (bf16[27,1,32]{2,0,1:T(8,128)(2,1)S(1)}, bf16[27,1,32]{2,0,1:T(8,128)(2,1)}, u32[]{:S(2)}) copy-start(bf16[27,1,32]{2,0,1:T(8,128)(2,1)} %param.9) | copy-start | bytes 5188
  22.9 1.4 %copy-start = (bf16[768,1536]{1,0:T(8,128)(2,1)}, bf16[768,1536]{1,0:T(8,128)(2,1)S(1)}, u32[]{:S(2)}) copy-start(bf16[768,1536]{1,0:T(8,128)(2,1)S(1)} %get-tuple-element.12.refs_11_) | copy-start | bytes 7077892

commit v2 on v0

--- a/solution.py
+++ b/solution.py
@@ -1,6 +1,8 @@
 import jax
 import jax.numpy as jnp
 from jax import lax
+from jax.experimental import pallas as pl
+from jax.experimental.pallas import tpu as pltpu
 from jax.sharding import PartitionSpec as P
 
 MID = 2
@@ -105,7 +107,7 @@
     )
 
 
-def shards(left_feat, right_feat, conv_first, conv_mid, conv_last):
+def general(left_feat, right_feat, conv_first, conv_mid, conv_last):
     piece_width = left_feat.shape[1]
     groups = conv_first.shape[2]
     disp_count = lax.axis_size("disp")
@@ -138,6 +140,445 @@
     return lax.dynamic_slice_in_dim(whole_row, lax.axis_index("disp") * piece_width, piece_width, 1)
 
 
+BF, F32 = jnp.bfloat16, jnp.float32
+NT = (((1,), (1,)), ((), ()))
+
+
+def dot(a, b, dims=(((1,), (0,)), ((), ()))):
+    return lax.dot_general(a, b, dims, preferred_element_type=F32)
+
+
+def iota(shape, dim):
+    return lax.broadcasted_iota(jnp.int32, shape, dim)
+
+
+def prep_kernel(perm_ref, cf_ref, cm_ref, cl_ref, w1_ref, wm_ref, wl_ref):
+    own = lax.axis_index("rows")
+
+    def strip(tap_of, a, h_in, eye):
+        rows = []
+        for e in (1, 0, -1):
+            for h_out in (0, 1):
+                rows.append(tap_of(9 * a + 3 * (h_in - h_out + 1) + (e + 1)))
+        rows.append(jnp.zeros((64, rows[0].shape[1]), BF))
+        return dot(eye, jnp.concatenate(rows, axis=0), NT)
+
+    def halves(base):
+        turned = pltpu.roll(base, 64, axis=1)
+        found = {1: base[:, :128], -1: base[:, 128:], 2: turned[:, :128], 0: turned[:, 128:]}
+        return {w_in: part.astype(BF) for w_in, part in found.items()}
+
+    def fill(ref, at, parts, rows, bases):
+        for d_in in (0, 1):
+            for w_in in range(-1, 3):
+                for base in bases:
+                    row = base + at(d_in, w_in)
+                    for place, rel in enumerate((0, 1, 2, -1)):
+                        a = d_in - rel + 1
+                        block = parts[a][w_in] if 0 <= a <= 2 else jnp.zeros((rows, 128), BF)
+                        ref[row : row + rows, 128 * place : 128 * place + 128] = block
+
+    def main_row(d_in, w_in):
+        return 128 * d_in + {0: 0, 1: 64, 2: 256, -1: 320}[w_in]
+
+    def rest_row(d_in, w_in):
+        return 512 + 32 * d_in + {0: 0, 1: 16, 2: 64, -1: 80}[w_in]
+
+    def eye_of(n):
+        return (iota((n, n), 0) == iota((n, n), 1)).astype(F32).astype(BF)
+
+    eye40, eye32 = eye_of(40), eye_of(32)
+    main, rest = [], []
+    for a in range(3):
+        parts = [strip(lambda t: cf_ref[t], a, h_in, eye40) for h_in in (0, 1)]
+        main.append(halves(jnp.concatenate([p[:32] for p in parts], axis=0)))
+        rest.append(halves(jnp.concatenate([p[32:] for p in parts], axis=0)))
+    fill(w1_ref, main_row, main, 64, (0,))
+    fill(w1_ref, rest_row, rest, 16, (0,))
+    for layer in range(2):
+        main = [
+            halves(
+                jnp.concatenate(
+                    [strip(lambda t: cm_ref[layer, t], a, h_in, eye32) for h_in in (0, 1)], axis=0
+                )
+            )
+            for a in range(3)
+        ]
+        fill(wm_ref.at[layer], main_row, main, 64, (0, 512))
+    clt = dot(eye32, cl_ref[...], NT).astype(BF)
+    lane = iota((27, 128), 1)
+    rel = jnp.where(lane < 32, 0, jnp.where(lane < 64, 2, jnp.where(lane < 96, 1, -1)))
+    for d_in in (0, 1):
+        for w_in in range(-1, 3):
+            for h_in in (0, 1):
+                a, e, b = d_in - rel, w_in - lane % 32, h_in - own
+                tap = 9 * (a + 1) + 3 * (b + 1) + (e + 1)
+                ok = (lane % 32 < 2) & (a >= -1) & (a <= 1) & (e >= -1) & (e <= 1) & (b >= -1) & (b <= 1)
+                pick = (ok & (iota((27, 128), 0) == tap)).astype(F32).astype(BF)
+                block = dot(clt, pick).astype(BF)
+                row = main_row(d_in, w_in) + 32 * h_in
+                wl_ref[row : row + 32] = block
+                wl_ref[512 + row : 544 + row] = block
+
+
+def perm_kernel(perm_ref):
+    own = lax.axis_index("rows")
+    lane = iota((1, 512), 1)
+    src = (((lane // 32) % 2) ^ own) * 320 + (lane % 32) * 8 + lane // 64
+    perm_ref[:, :512] = (iota((640, 512), 0) == src).astype(F32).astype(BF)
+    lane = iota((1, 512), 1)
+    src = (((lane // 8) % 2) ^ own) * 320 + (32 + lane % 8) * 8 + (lane // 128) * 2 + (lane // 64) % 2
+    perm_ref[:, 512:] = (iota((640, 512), 0) == src).astype(F32).astype(BF)
+
+
+def prep(cf, cm, cl):
+    vm = pl.BlockSpec(memory_space=pltpu.VMEM)
+    perm = pl.pallas_call(
+        perm_kernel,
+        out_shape=jax.ShapeDtypeStruct((640, 1024), BF),
+        out_specs=vm,
+        compiler_params=pltpu.CompilerParams(vmem_limit_bytes=8 * 2**20),
+        cost_estimate=pl.CostEstimate(flops=10**9, bytes_accessed=3 * 10**6, transcendentals=0),
+        name="perm",
+    )()
+    ws = pl.pallas_call(
+        prep_kernel,
+        out_shape=(
+            jax.ShapeDtypeStruct((640, 512), BF),
+            jax.ShapeDtypeStruct((2, 1024, 512), BF),
+            jax.ShapeDtypeStruct((1024, 128), BF),
+        ),
+        in_specs=[vm] * 4,
+        out_specs=[vm] * 3,
+        compiler_params=pltpu.CompilerParams(vmem_limit_bytes=16 * 2**20),
+        cost_estimate=pl.CostEstimate(flops=2 * 10**9, bytes_accessed=4 * 10**6, transcendentals=0),
+        name="prep",
+    )(perm, cf, cm, cl)
+    return (*ws, perm)
+
+
+def main_body(load_r, load_l, w1_ref, wm_ref, wl_ref, perm_ref, out_ref, win, rs, lp, xb1, xb, xb2, xb3):
+    z = lax.axis_index("disp")
+    core = lax.axis_index("cols")
+    piece = core * 4 + z
+    win[...] = jnp.zeros_like(win)
+
+    def put(row, part):
+        win[row : row + part.shape[0]] = part
+
+    put(0, load_r(1, 0, 16))
+    put(16, load_r(-3, 16, 32))
+    put(32, load_r(-2, 0, 32))
+    put(64, load_r(-1, 0, 32))
+    put(96, load_r(0, 0, 32))
+    put(136, load_l(-1))
+    put(144, load_l(0))
+    put(176, load_l(1))
+    zp = dot(win[...], perm_ref[...])
+    halfway = iota((128, 128), 1) < 64
+    near_half, far_half = [], []
+    for tile in range(4):
+        straight = zp[:, 128 * tile : 128 * tile + 128]
+        turned = pltpu.roll(straight, 64, axis=1)
+        for even, a, b in ((0, straight, turned), (1, turned, straight)):
+            near_half.append(jnp.where(halfway, a[:128], 0.0).astype(BF))
+            far_half.append(jnp.where(halfway, 0.0, b[:128]).astype(BF))
+            lp[2 * tile + even] = jnp.where(halfway[:64], a[128:], b[128:])
+    for tile in range(4):
+        lp[8 + tile] = zp[128:, 512 + 128 * tile : 640 + 128 * tile]
+    zm = jnp.concatenate(
+        [jnp.concatenate(near_half, axis=1), jnp.concatenate(far_half, axis=1)], axis=0
+    )
+    zpr = zp[:128]
+    lane = iota((128, 512), 1)
+    ze = jnp.concatenate(
+        [jnp.where((lane // 16) % 4 == ww, zpr[:, 512:], 0.0).astype(BF) for ww in range(4)], axis=0
+    )
+    s, q = iota((112, 256), 0), iota((112, 256), 1)
+    r = q % 128
+    rel = jnp.where(r < 16, 32 + r, r - 96)
+    dd = jnp.where(s < 56, 0, 1)
+    pick = (rel == 36 + q // 128 - dd - 2 * (s - 56 * dd)).astype(F32).astype(BF)
+    rsm = dot(pick, zm)
+    s, q = iota((56, 512), 0), iota((56, 512), 1)
+    r = q % 128
+    rel = jnp.where(r < 16, 32 + r, r - 96)
+    pick = (rel == 36 + (q // 128) % 2 - q // 256 - 2 * s).astype(F32).astype(BF)
+    rse = dot(pick, ze)
+    for tile in range(8):
+        rs[tile] = rsm[:, 128 * tile : 128 * tile + 128]
+    for tile in range(4):
+        rs[8 + tile, 0:56] = rse[:, 128 * tile : 128 * tile + 128]
+
+    def left_row(tile, column):
+        for first, row in ((36, 48), (4, 16), (0, 12)):
+            if column >= first:
+                at = row + column - first
+                return lp[tile, at : at + 1]
+
+    lane = iota((32, 128), 1)
+    low, even = lane < 64, (lane // 16) % 2 == 0
+    depth = iota((32, 128), 0)
+    nothing = jnp.zeros((32, 128), BF)
+    first_ok = piece > 0
+    last_ok = piece < 4 * lax.axis_size("cols") - 1
+
+    def before(tile):
+        return jnp.where(depth == 0, 0.0, pltpu.roll(tile, 1, axis=0))
+
+    def after(tile):
+        return jnp.where(depth == 31, 0.0, pltpu.roll(tile, 31, axis=0))
+
+    class Rows:
+        def __init__(self, out, own_lanes, halo_lanes, pick):
+            self.out, self.own, self.halo, self.pick = out, own_lanes, halo_lanes, pick
+            self.last, self.prior = None, None
+
+        def push(self, block, values):
+            if self.last is not None:
+                self._halo(block - 1, values)
+            here = slice(32 * block, 32 * block + 32)
+            if self.own is not None:
+                for lanes, value in zip(self.own, values):
+                    self.out[here, lanes : lanes + 128] = value
+            self.prior, self.last = self.last, values
+            self.block = block
+
+        def end(self):
+            self._halo(self.block, [nothing] * len(self.last))
+
+        def _halo(self, block, following):
+            here = slice(32 * block, 32 * block + 32)
+            prior = self.prior or [nothing] * len(following)
+            for lanes, a, b, c in zip(self.halo, prior, self.last, following):
+                self.out[here, lanes : lanes + 128] = self.pick(a, b, c)
+
+    def beside(a, b, c):
+        return jnp.where(low, c, a)
+
+    def around(a, b, c):
+        return jnp.where(low, b, jnp.where(even, c, a))
+
+    volume = Rows(xb1, (0, 128), (256, 384), beside)
+    remainder = Rows(xb1, None, (512,), around)
+    for w2 in range(20):
+        start = 20 - w2
+        tiles = []
+        for dd in range(2):
+            acc = None
+            for c in range(8):
+                left = jnp.where(low, left_row(c, 2 * w2), left_row(c, 2 * w2 + 1))
+                term = left * rs[c, 56 * dd + start : 56 * dd + start + 32]
+                acc = term if acc is None else acc + term
+            tiles.append(acc * 0.125)
+        acc = None
+        for c in range(4):
+            left = jnp.where(even, left_row(8 + c, 2 * w2), left_row(8 + c, 2 * w2 + 1))
+            term = left * rs[8 + c, start : start + 32]
+            acc = term if acc is None else acc + term
+        rest = (acc + pltpu.roll(acc, 64, axis=1)) * 0.125
+        volume.push(w2, [tile.astype(BF) for tile in tiles])
+        remainder.push(w2, [rest.astype(BF)])
+    volume.end()
+    remainder.end()
+
+
+    class Layer:
+        def __init__(self, x, weights, out, cuts):
+            own = (0, 128, 512, 640)
+            self.rows = Rows(out, own, [lanes + 256 for lanes in own], beside)
+            self.x, self.weights = x, weights
+            self.chunks = list(zip(cuts, cuts[1:]))
+
+        def step(self):
+            first, stop = self.chunks.pop(0)
+            y = dot(self.x[32 * first : 32 * stop], self.weights[...])
+            for w2 in range(first, stop):
+                here = y[32 * (w2 - first) : 32 * (w2 - first) + 32]
+                tiles = [
+                    here[:, :128] + before(here[:, 256:384]),
+                    here[:, 128:256] + after(here[:, 384:]),
+                ]
+                tiles = [jnp.maximum(tile, 0.0) for tile in tiles]
+                if w2 < 2:
+                    tiles = [jnp.where(first_ok, tile, 0.0) for tile in tiles]
+                if w2 > 17:
+                    tiles = [jnp.where(last_ok, tile, 0.0) for tile in tiles]
+                high = [tile.astype(BF) for tile in tiles]
+                rest = [(tile - part.astype(F32)).astype(BF) for tile, part in zip(tiles, high)]
+                self.rows.push(w2, high + rest)
+            if not self.chunks:
+                self.rows.end()
+
+    layers = [
+        Layer(xb1, w1_ref, xb, (0, 7, 14, 20)),
+        Layer(xb, wm_ref.at[0], xb2, (1, 6, 13, 19)),
+        Layer(xb2, wm_ref.at[1], xb3, (1, 5, 12, 19)),
+    ]
+    for each in layers:
+        for _ in range(len(each.chunks)):
+            each.step()
+    y = dot(xb3[64:576], wl_ref[...])
+    cost = jnp.zeros((32, 128), F32)
+    for w2 in range(16):
+        part = y[32 * w2 : 32 * w2 + 32]
+        part = part if w2 == 0 else pltpu.roll(part, 2 * w2, axis=1)
+        cost = jnp.where((lane % 32) // 2 == w2, part, cost)
+    moved = jnp.where(low, before(cost), after(cost))
+    cost = cost + pltpu.roll(moved, 96, axis=1)
+    top = jnp.max(cost, axis=0, keepdims=True)
+    top = jnp.maximum(top, pltpu.roll(top, 64, axis=1))
+    weight = jnp.exp(cost - top)
+    level = (2 * depth + jnp.where(low, 0, 1)).astype(F32) * (1.0 / 64)
+    upper = jnp.sum(weight * level, axis=0, keepdims=True)
+    under = jnp.sum(weight, axis=0, keepdims=True)
+    est = (upper + pltpu.roll(upper, 64, axis=1)) / (under + pltpu.roll(under, 64, axis=1))
+    out_ref[...] = est[:, :32]
+
+
+SCRATCH = [
+    pltpu.VMEM((192, 640), BF),
+    pltpu.VMEM((12, 112, 128), F32),
+    pltpu.VMEM((12, 64, 128), F32),
+    pltpu.VMEM((640, 640), BF),
+    pltpu.VMEM((640, 1024), BF),
+    pltpu.VMEM((640, 1024), BF),
+    pltpu.VMEM((640, 1024), BF),
+]
+
+
+def joined(out_ref, first, s_ref, t_ref):
+    for half, ref in enumerate((s_ref, t_ref)):
+        lanes = slice(320 * half, 320 * half + 320)
+        left = ref[1]
+        out_ref[first + (slice(0, 32), lanes)] = ref[0]
+        out_ref[first + (slice(32, 40), lanes)] = jnp.concatenate([left[:4], left[28:]], axis=0)
+
+
+def pack_kernel(s_ref, t_ref, own_ref, edge_ref, rights_ref):
+    joined(edge_ref, (), s_ref, t_ref)
+    for half, ref in enumerate((s_ref, t_ref)):
+        lanes = slice(320 * half, 320 * half + 320)
+        own_ref[0:32, lanes] = ref[0]
+        own_ref[32:64, lanes] = ref[1]
+        rights_ref[:, lanes] = ref[0]
+
+
+def pack(s, t):
+    vm = pl.BlockSpec(memory_space=pltpu.VMEM)
+    return pl.pallas_call(
+        pack_kernel,
+        out_shape=[jax.ShapeDtypeStruct((rows, 640), BF) for rows in (64, 40, 32)],
+        in_specs=[vm] * 2,
+        out_specs=[vm] * 3,
+        compiler_params=pltpu.CompilerParams(vmem_limit_bytes=2**20),
+        name="pack",
+    )(s, t)
+
+
+def collect_kernel(one_ref, two_ref, s_ref, t_ref, out_ref):
+    out_ref[0] = one_ref[...]
+    out_ref[1, 0:32] = two_ref[...]
+    out_ref[1, 32:40] = jnp.zeros((8, 640), BF)
+    joined(out_ref, (2,), s_ref, t_ref)
+
+
+def collect(*parts):
+    vm = pl.BlockSpec(memory_space=pltpu.VMEM)
+    return pl.pallas_call(
+        collect_kernel,
+        out_shape=jax.ShapeDtypeStruct((3, 40, 640), BF),
+        in_specs=[vm] * 4,
+        out_specs=vm,
+        compiler_params=pltpu.CompilerParams(vmem_limit_bytes=2**20),
+        name="collect",
+    )(*parts)
+
+
+def stage_kernel(s_ref, out_ref):
+    out_ref[...] = s_ref[...]
+
+
+def stage(s):
+    vm = pl.BlockSpec(memory_space=pltpu.VMEM)
+    return pl.pallas_call(
+        stage_kernel,
+        out_shape=jax.ShapeDtypeStruct(s.shape, BF),
+        in_specs=[vm],
+        out_specs=vm,
+        compiler_params=pltpu.CompilerParams(vmem_limit_bytes=2**20),
+        cost_estimate=pl.CostEstimate(flops=10**9, bytes_accessed=10**6, transcendentals=0),
+        name="stage",
+    )(s)
+
+
+def main_kernel(own, other, near, far, w1, wm, wl, perm, out, win, rs, lp, xb1, xb, xb2, xb3):
+    z, core = lax.axis_index("disp"), lax.axis_index("cols")
+    piece = core * 4 + z
+
+    def load(dp, lo, hi):
+        row = jnp.where(iota((hi - lo, 640), 1) < 320, 0, 1)
+        if dp == 0:
+            return jnp.where(row == 0, own[lo:hi], other[lo:hi])
+        want = piece + dp
+        ok = (want >= 0) & (want < 8)
+        want = jnp.clip(want, 0, 7)
+        turn = jnp.maximum((z ^ (want % 4)) - 1, 0)
+        flip = core ^ (want // 4)
+        part = jnp.where(row == flip, far[turn, lo:hi], near[turn, lo:hi])
+        return jnp.where(ok, part, jnp.zeros((), BF))
+
+    def left(dp):
+        return load(dp, 32, 64) if dp == 0 else load(dp, 32, 40)
+
+    main_body(load, left, w1, wm, wl, perm, out, win, rs, lp, xb1, xb, xb2, xb3)
+
+
+def crossed(v, axis, k):
+    count = lax.axis_size(axis)
+    pairs = [(2 * i + c, 2 * (i ^ k) + 1 - c) for i in range(count) for c in (0, 1)]
+    return lax.ppermute(v, (axis, "cols"), pairs)
+
+
+def fast(left_feat, right_feat, conv_first, conv_mid, conv_last):
+    zero = jnp.zeros((), BF)
+    none = (0, 0, 0)
+    s = lax.pad(right_feat, zero, ((0, 1, 0), none, none)) + lax.pad(
+        left_feat, zero, ((1, 0, 0), none, none)
+    )
+    t = crossed(s, "rows", 1)
+    s_3 = crossed(stage(s), "disp", 3)
+    own, edge, rights = pack(s, t)
+    swap = [(0, 1), (1, 0)]
+    from_1 = crossed(edge, "disp", 1)
+    from_2 = crossed(rights, "disp", 2)
+    t_3 = crossed(s_3, "rows", 1)
+    ws = prep(conv_first, conv_mid, conv_last.reshape(27, 32))
+    other = lax.ppermute(own, "cols", swap)
+    ws, from_1, from_2, s_3, t_3, other = lax.optimization_barrier(
+        (ws, from_1, from_2, s_3, t_3, other)
+    )
+    near = collect(from_1, from_2, s_3, t_3)
+    far = lax.ppermute(near, "cols", swap)
+    vm = pl.BlockSpec(memory_space=pltpu.VMEM)
+    return pl.pallas_call(
+        main_kernel,
+        out_shape=jax.ShapeDtypeStruct((1, 32), F32),
+        in_specs=[vm] * 8,
+        out_specs=vm,
+        scratch_shapes=SCRATCH,
+        compiler_params=pltpu.CompilerParams(vmem_limit_bytes=24 * 2**20),
+        name="cost_volume",
+    )(own, other, near, far, *ws)
+
+
+def shards(left_feat, right_feat, conv_first, conv_mid, conv_last):
+    sizes = tuple(lax.axis_size(name) for name in ("disp", "rows", "cols"))
+    if sizes == (4, 2, 2) and left_feat.shape == (1, 32, 320) and conv_first.shape == (27, 32, 40):
+        return fast(left_feat, right_feat, conv_first, conv_mid, conv_last)
+    return general(left_feat, right_feat, conv_first, conv_mid, conv_last)
+
+
 def solution(mesh):
     return jax.shard_map(
         shards,

time: 224 us -> 20 us (0.09)
  blocking collectives: 57.6 us -> 0 us
  starting transfers between devices: 53.4 us -> 11.3 us
  waiting for transfers between devices: 40.8 us -> 2.11 us
  local copies, waits for them, and re-layouts: 35.7 us -> 0.02 us
  other arithmetic: 13.7 us -> 0.77 us
  loops' own time: 10.9 us -> 0 us
  matrix products: 9.94 us -> 0 us
  Pallas kernels: 0 us -> 5.56 us
    all_gather x5 -> x0, blocking collectives: 57.6 us -> none  [the longest x3 28.7 us: combined_all(): gathered = jax.tree.map(lambda a: lax.all_gather(a, axis), part)]
    ppermute x25 -> x7, starting transfers between devices: 53.4 us -> 11.3 us  [the longest x5 10.7 us: crossed(): return lax.ppermute(v, (axis, 'cols'), pairs)]
    ppermute x25 -> x7, waiting for transfers between devices: 40.8 us -> 2.11 us  [the longest x5 1.1 us: crossed(): return lax.ppermute(v, (axis, 'cols'), pairs)]
    dynamic_slice x17 -> x0, local copies, waits for them, and re-layouts: 11 us -> none  [the longest x16 10.4 us: correlate(): return lax.map(single, jnp.arange(count, dtype=jnp.int32))]
    ppermute x8 -> x0, local copies, waits for them, and re-layouts: 11 us -> none  [the longest x4 6.55 us: extended_2(): lax.ppermute(lax.slice_in_dim(block, 0, width, axis=dim), axis, backward)]
    another operation x2 -> x0, loops' own time: 10.9 us -> none  [the longest x1 10.8 us: correlate(): return lax.map(single, jnp.arange(count, dtype=jnp.int32))]
    dot_general x12 -> x0, matrix products: 9.94 us -> none  [convolve(): jnp.einsum('ok,dkn->don', taps, flat[disp_tap:disp_tap + depth_out], pref...]
    unnamed x24 -> x0, other arithmetic: 9.72 us -> none
  transfers between devices with their start and end apart: 25 -> 7, of which waited for: 14 -> 2; matrix products, arithmetic and copies ran while one was open for 8% -> 0% of each run, Pallas kernels for 0% -> 6%
where the time goes in v2:
time: 20 us; the launch traced here: 19.8 us
  starting transfers between devices  11.3 us (56%)
  Pallas kernels  5.56 us (28%)
  waiting for transfers between devices  2.11 us (11%)
  other arithmetic  0.77 us (4%)
    ppermute x5, starting transfers between devices, crossed(): return lax.ppermute(v, (axis, 'cols'), pairs)  10.7 us
    pallas_call x1, Pallas kernels, fast(): pl.pallas_call(main_kernel, out_shape=jax.ShapeDtypeStruct((1, 32), F32),...  4.25 us
    ppermute x5, waiting for transfers between devices, crossed(): return lax.ppermute(v, (axis, 'cols'), pairs)  1.1 us
    ppermute x1, waiting for transfers between devices, fast(): far = lax.ppermute(near, 'cols', swap)  1.02 us
    pallas_call x1, Pallas kernels, prep(): pl.pallas_call(prep_kernel, out_shape=(jax.ShapeDtypeStruct((640, 512), B...  0.84 us
    add x1, other arithmetic, fast(): lax.pad(right_feat, zero, ((0, 1, 0), none, none))  0.77 us
    ppermute x1, starting transfers between devices, fast(): far = lax.ppermute(near, 'cols', swap)  0.51 us
  transfers between devices with their start and end apart: 7, of which 2 were waited for; matrix products, arithmetic and copies ran while one was open for 0% of the time, Pallas kernels for 6%

profile of v2, /device:TPU:0, one launch (start us, length us, event | category | flops | bytes accessed | tf_op | source)
XLA Modules:
  0.0 19.8 jit_solution(17357197898385161099)
XLA Ops:
  0.0 0.8 %pad_add_fusion.s_ref = bf16[2,32,320]{2,1,0:T(8,128)(2,1)S(1)} fusion(bf16[1,32,320]{2,1,0:T(8,128)(2,1)} %param.5, bf16[1,32,320]{2,1,0:T(8,128)(2,1)} %param.6), kind=kLoop, calls=%fused_computation | loop fusion | flops 20480 | bytes 81920 | tf_op jit(solution)/shard_map/add | solution.py:546
  0.8 2.4 %collective-permute-start = (bf16[2,32,320]{2,1,0:T(8,128)(2,1)S(1)}, bf16[2,32,320]{2,1,0:T(8,128)(2,1)S(1)}, u32[]{:S(2)}, u32[]{:S(2)}) collective-permute-start(bf16[2,32,320]{2,1,0:T(8,128)(2,1)S(1)} %pad_add_fusion.s_ref), channel_id=1, source_target_pairs={{0,3},{1,2},{2,1},{3,0},{4,7},{5,6},{6,5},{7,4},{8,11},{9,10},{10,... | collective-permute-start | bytes 122888 | tf_op jit(solution)/shard_map/ppermute | solution.py:540
  3.2 0.0 copy-start.1
  3.2 0.0 copy-start.2
  3.2 3.9 %collective-permute-start.3 = (bf16[2,32,320]{2,1,0:T(8,128)(2,1)S(1)}, bf16[2,32,320]{2,1,0:T(8,128)(2,1)S(1)}, u32[]{:S(2)}, u32[]{:S(2)}) collective-permute-start(bf16[2,32,320]{2,1,0:T(8,128)(2,1)S(1)} %stage.1), channel_id=1, source_target_pairs={{0,13},{1,12},{4,9},{5,8},{8,5},{9,4},{12,1},{13,0},{2,15},{3,14},... | collective-permute-start | bytes 122888 | tf_op jit(solution)/shard_map/ppermute | solution.py:540
  7.2 0.3 %perm.1.perm_ref = bf16[640,1024]{1,0:T(8,128)(2,1)S(1)} custom-call(), custom_call_target="tpu_custom_call" | custom-call | flops 1000000000 | bytes 3000000 | tf_op jit(solution)/shard_map/perm/pallas_call | solution.py:236
  7.5 0.0 collective-permute-done.t_ref
  7.5 0.1 pack.1
  7.6 1.2 %collective-permute-start.2 = (bf16[32,640]{1,0:T(8,128)(2,1)S(1)}, bf16[32,640]{1,0:T(8,128)(2,1)S(1)}, u32[]{:S(2)}, u32[]{:S(2)}) collective-permute-start(bf16[32,640]{1,0:T(8,128)(2,1)S(1)} %get-tuple-element.25), channel_id=1, source_target_pairs={{0,9},{1,8},{4,13},{5,12},{8,1},{9,0},{12,5},{13,4},{2,11},{3,10},... | collective-permute-start | bytes 122888 | tf_op jit(solution)/shard_map/ppermute | solution.py:540
  8.8 1.6 %collective-permute-start.1 = (bf16[40,640]{1,0:T(8,128)(2,1)S(1)}, bf16[40,640]{1,0:T(8,128)(2,1)S(1)}, u32[]{:S(2)}, u32[]{:S(2)}) collective-permute-start(bf16[40,640]{1,0:T(8,128)(2,1)S(1)} %get-tuple-element.24), channel_id=1, source_target_pairs={{0,5},{1,4},{4,1},{5,0},{8,13},{9,12},{12,9},{13,8},{2,7},{3,6},{6... | collective-permute-start | bytes 153608 | tf_op jit(solution)/shard_map/ppermute | solution.py:540
  10.4 0.1 collective-permute-start.5
  10.4 0.0 collective-permute-done.3.s_ref
  10.5 1.6 %collective-permute-start.4 = (bf16[2,32,320]{2,1,0:T(8,128)(2,1)S(1)}, bf16[2,32,320]{2,1,0:T(8,128)(2,1)S(1)}, u32[]{:S(2)}, u32[]{:S(2)}) collective-permute-start(bf16[2,32,320]{2,1,0:T(8,128)(2,1)S(1)} %collective-permute-done.3.s_ref), channel_id=1, source_target_pairs={{0,3},{1,2},{2,1},{3,0},{4,7},{5,6},{6,5},{7,4},{8,11},{9,10},{10,... | collective-permute-start | bytes 122888 | tf_op jit(solution)/shard_map/ppermute | solution.py:540
  12.0 0.0 copy-done
  12.0 0.0 copy-done.2
  12.0 0.8 %prep.1 = (bf16[640,512]{1,0:T(8,128)(2,1)S(1)}, bf16[2,1024,512]{2,1,0:T(8,128)(2,1)S(1)}, bf16[1024,128]{1,0:T(8,128)(2,1)S(1)}) custom-call(bf16[640,1024]{1,0:T(8,128)(2,1)S(1)} %perm.1.perm_ref, bf16[27,32,40]{2,1,0:T(8,128)(2,1)S(1)} %copy-done.1, bf16[2,27,32,32]{3,2,1,0:T(8,128)(2,1)S(1)} %copy-done, bf16[27,32]{1,0:T(8,128)(2,1)S(1)} %bitcast.1), custom_call_target="tpu_custom_call" | custom-call | flops 2000000000 | bytes 4000000 | tf_op jit(solution)/shard_map/prep/pallas_call | solution.py:244
  12.9 1.1 %collective-permute-done.4.t_ref = bf16[2,32,320]{2,1,0:T(8,128)(2,1)S(1)} collective-permute-done((bf16[2,32,320]{2,1,0:T(8,128)(2,1)S(1)}, bf16[2,32,320]{2,1,0:T(8,128)(2,1)S(1)}, u32[]{:S(2)}, u32[]{:S(2)}) %collective-permute-start.4) | collective-permute-done | bytes 40992 | tf_op jit(solution)/shard_map/ppermute | solution.py:540
  14.0 0.0 collective-permute-done.2.two_ref
  14.0 0.0 collective-permute-done.1.one_ref
  14.0 0.0 collective-permute-done.5.other
  14.0 0.1 collect.1.near
  14.1 0.5 %collective-permute-start.6 = (bf16[3,40,640]{2,1,0:T(8,128)(2,1)S(1)}, bf16[3,40,640]{2,1,0:T(8,128)(2,1)S(1)}, u32[]{:S(2)}, u32[]{:S(2)}) collective-permute-start(bf16[3,40,640]{2,1,0:T(8,128)(2,1)S(1)} %collect.1.near), channel_id=1, source_target_pairs={{0,1},{1,0},{2,3},{3,2},{4,5},{5,4},{6,7},{7,6},{8,9},{9,8},{10,11... | collective-permute-start | bytes 460808 | tf_op jit(solution)/shard_map/ppermute | solution.py:562
  14.6 1.0 %collective-permute-done.6.far = bf16[3,40,640]{2,1,0:T(8,128)(2,1)S(1)} collective-permute-done((bf16[3,40,640]{2,1,0:T(8,128)(2,1)S(1)}, bf16[3,40,640]{2,1,0:T(8,128)(2,1)S(1)}, u32[]{:S(2)}, u32[]{:S(2)}) %collective-permute-start.6) | collective-permute-done | bytes 153632 | tf_op jit(solution)/shard_map/ppermute | solution.py:562
  15.6 4.3 %cost_volume.1 = f32[1,32]{1,0:T(1,128)} custom-call(bf16[64,640]{1,0:T(8,128)(2,1)S(1)} %get-tuple-element.20.own, bf16[64,640]{1,0:T(8,128)(2,1)S(1)} %collective-permute-done.5.other, bf16[3,40,640]{2,1,0:T(8,128)(2,1)S(1)} %collect.1.near, bf16[3,40,640]{2,1,0:T(8,128)(2,1)S(1)} %collective-permute-done.6.far, ...), custom_call_target="tpu_custom_call" | custom-call | tf_op jit(solution)/shard_map/cost_volume/pallas_call | solution.py:564
  (3 shorter events, 0.0 us)
Async XLA Ops:
  0.8 6.7 %collective-permute-start = (bf16[2,32,320]{2,1,0:T(8,128)(2,1)S(1)}, bf16[2,32,320]{2,1,0:T(8,128)(2,1)S(1)}, u32[]{:S(2)}, u32[]{:S(2)}) collective-permute-start(bf16[2,32,320]{2,1,0:T(8,128)(2,1)S(1)} %pad_add_fusion.s_ref), channel_id=1, source_target_pairs={{0,3},{1,2},{2,1},{3,0},{4,7},{5,6},{6,5},{7,4},{8,11},{9,10},{10,... | collective-permute-start | bytes 122888 | tf_op jit(solution)/shard_map/ppermute | solution.py:540
  3.2 8.8 %copy-start = (bf16[2,27,32,32]{3,2,1,0:T(8,128)(2,1)S(1)}, bf16[2,27,32,32]{3,2,1,0:T(8,128)(2,1)}, u32[]{:S(2)}) copy-start(bf16[2,27,32,32]{3,2,1,0:T(8,128)(2,1)} %cm_ref.1) | copy-start | bytes 331780
  3.2 8.8 %copy-start.1 = (bf16[27,32,40]{2,1,0:T(8,128)(2,1)S(1)}, bf16[27,32,40]{2,1,0:T(8,128)(2,1)}, u32[]{:S(2)}) copy-start(bf16[27,32,40]{2,1,0:T(8,128)(2,1)} %cf_ref.1) | copy-start | bytes 207364
  3.2 8.8 %copy-start.2 = (bf16[27,1,32]{2,0,1:T(8,128)(2,1)S(1)}, bf16[27,1,32]{2,0,1:T(8,128)(2,1)}, u32[]{:S(2)}) copy-start(bf16[27,1,32]{2,0,1:T(8,128)(2,1)} %param.9) | copy-start | bytes 5188
  3.2 7.2 %collective-permute-start.3 = (bf16[2,32,320]{2,1,0:T(8,128)(2,1)S(1)}, bf16[2,32,320]{2,1,0:T(8,128)(2,1)S(1)}, u32[]{:S(2)}, u32[]{:S(2)}) collective-permute-start(bf16[2,32,320]{2,1,0:T(8,128)(2,1)S(1)} %stage.1), channel_id=1, source_target_pairs={{0,13},{1,12},{4,9},{5,8},{8,5},{9,4},{12,1},{13,0},{2,15},{3,14},... | collective-permute-start | bytes 122888 | tf_op jit(solution)/shard_map/ppermute | solution.py:540
  7.6 6.4 %collective-permute-start.2 = (bf16[32,640]{1,0:T(8,128)(2,1)S(1)}, bf16[32,640]{1,0:T(8,128)(2,1)S(1)}, u32[]{:S(2)}, u32[]{:S(2)}) collective-permute-start(bf16[32,640]{1,0:T(8,128)(2,1)S(1)} %get-tuple-element.25), channel_id=1, source_target_pairs={{0,9},{1,8},{4,13},{5,12},{8,1},{9,0},{12,5},{13,4},{2,11},{3,10},... | collective-permute-start | bytes 122888 | tf_op jit(solution)/shard_map/ppermute | solution.py:540
  8.8 5.2 %collective-permute-start.1 = (bf16[40,640]{1,0:T(8,128)(2,1)S(1)}, bf16[40,640]{1,0:T(8,128)(2,1)S(1)}, u32[]{:S(2)}, u32[]{:S(2)}) collective-permute-start(bf16[40,640]{1,0:T(8,128)(2,1)S(1)} %get-tuple-element.24), channel_id=1, source_target_pairs={{0,5},{1,4},{4,1},{5,0},{8,13},{9,12},{12,9},{13,8},{2,7},{3,6},{6... | collective-permute-start | bytes 153608 | tf_op jit(solution)/shard_map/ppermute | solution.py:540
  10.4 3.6 %collective-permute-start.5 = (bf16[64,640]{1,0:T(8,128)(2,1)S(1)}, bf16[64,640]{1,0:T(8,128)(2,1)S(1)}, u32[]{:S(2)}, u32[]{:S(2)}) collective-permute-start(bf16[64,640]{1,0:T(8,128)(2,1)S(1)} %get-tuple-element.20.own), channel_id=1, source_target_pairs={{0,1},{1,0},{2,3},{3,2},{4,5},{5,4},{6,7},{7,6},{8,9},{9,8},{10,11... | collective-permute-start | bytes 245768 | tf_op jit(solution)/shard_map/ppermute | solution.py:557
  10.5 3.5 %collective-permute-start.4 = (bf16[2,32,320]{2,1,0:T(8,128)(2,1)S(1)}, bf16[2,32,320]{2,1,0:T(8,128)(2,1)S(1)}, u32[]{:S(2)}, u32[]{:S(2)}) collective-permute-start(bf16[2,32,320]{2,1,0:T(8,128)(2,1)S(1)} %collective-permute-done.3.s_ref), channel_id=1, source_target_pairs={{0,3},{1,2},{2,1},{3,0},{4,7},{5,6},{6,5},{7,4},{8,11},{9,10},{10,... | collective-permute-start | bytes 122888 | tf_op jit(solution)/shard_map/ppermute | solution.py:540
  14.1 1.5 %collective-permute-start.6 = (bf16[3,40,640]{2,1,0:T(8,128)(2,1)S(1)}, bf16[3,40,640]{2,1,0:T(8,128)(2,1)S(1)}, u32[]{:S(2)}, u32[]{:S(2)}) collective-permute-start(bf16[3,40,640]{2,1,0:T(8,128)(2,1)S(1)} %collect.1.near), channel_id=1, source_target_pairs={{0,1},{1,0},{2,3},{3,2},{4,5},{5,4},{6,7},{7,6},{8,9},{9,8},{10,11... | collective-permute-start | bytes 460808 | tf_op jit(solution)/shard_map/ppermute | solution.py:562

commit v3 on v2

--- a/solution.py
+++ b/solution.py
@@ -447,21 +447,15 @@
 ]
 
 
-def joined(out_ref, first, s_ref, t_ref):
+def pack_kernel(s_ref, t_ref, own_ref, edge_ref, rights_ref):
     for half, ref in enumerate((s_ref, t_ref)):
         lanes = slice(320 * half, 320 * half + 320)
-        left = ref[1]
-        out_ref[first + (slice(0, 32), lanes)] = ref[0]
-        out_ref[first + (slice(32, 40), lanes)] = jnp.concatenate([left[:4], left[28:]], axis=0)
-
-
-def pack_kernel(s_ref, t_ref, own_ref, edge_ref, rights_ref):
-    joined(edge_ref, (), s_ref, t_ref)
-    for half, ref in enumerate((s_ref, t_ref)):
-        lanes = slice(320 * half, 320 * half + 320)
-        own_ref[0:32, lanes] = ref[0]
-        own_ref[32:64, lanes] = ref[1]
-        rights_ref[:, lanes] = ref[0]
+        right, left = ref[:, :320], ref[:, 320:]
+        edge_ref[0:32, lanes] = right
+        edge_ref[32:40, lanes] = jnp.concatenate([left[:4], left[28:]], axis=0)
+        own_ref[0:32, lanes] = right
+        own_ref[32:64, lanes] = left
+        rights_ref[:, lanes] = right
 
 
 def pack(s, t):
@@ -480,7 +474,8 @@
     out_ref[0] = one_ref[...]
     out_ref[1, 0:32] = two_ref[...]
     out_ref[1, 32:40] = jnp.zeros((8, 640), BF)
-    joined(out_ref, (2,), s_ref, t_ref)
+    out_ref[2, :, 0:320] = s_ref[...]
+    out_ref[2, :, 320:640] = t_ref[...]
 
 
 def collect(*parts):
@@ -496,14 +491,16 @@
 
 
 def stage_kernel(s_ref, out_ref):
-    out_ref[...] = s_ref[...]
+    left = s_ref[:, 320:]
+    out_ref[0:32] = s_ref[:, :320]
+    out_ref[32:40] = jnp.concatenate([left[:4], left[28:]], axis=0)
 
 
 def stage(s):
     vm = pl.BlockSpec(memory_space=pltpu.VMEM)
     return pl.pallas_call(
         stage_kernel,
-        out_shape=jax.ShapeDtypeStruct(s.shape, BF),
+        out_shape=jax.ShapeDtypeStruct((40, 320), BF),
         in_specs=[vm],
         out_specs=vm,
         compiler_params=pltpu.CompilerParams(vmem_limit_bytes=2**20),
@@ -542,9 +539,8 @@
 
 def fast(left_feat, right_feat, conv_first, conv_mid, conv_last):
     zero = jnp.zeros((), BF)
-    none = (0, 0, 0)
-    s = lax.pad(right_feat, zero, ((0, 1, 0), none, none)) + lax.pad(
-        left_feat, zero, ((1, 0, 0), none, none)
+    s = lax.pad(right_feat[0], zero, ((0, 0, 0), (0, 320, 0))) + lax.pad(
+        left_feat[0], zero, ((0, 0, 0), (320, 0, 0))
     )
     t = crossed(s, "rows", 1)
     s_3 = crossed(stage(s), "disp", 3)
@@ -552,9 +548,10 @@
     swap = [(0, 1), (1, 0)]
     from_1 = crossed(edge, "disp", 1)
     from_2 = crossed(rights, "disp", 2)
+    other = lax.ppermute(own, "cols", swap)
+    s_3, other = lax.optimization_barrier((s_3, other))
     t_3 = crossed(s_3, "rows", 1)
     ws = prep(conv_first, conv_mid, conv_last.reshape(27, 32))
-    other = lax.ppermute(own, "cols", swap)
     ws, from_1, from_2, s_3, t_3, other = lax.optimization_barrier(
         (ws, from_1, from_2, s_3, t_3, other)
     )

time: 20 us -> 19.9 us (level)
  transfers between devices with their start and end apart: 7 -> 7, of which waited for: 2 -> 4; matrix products, arithmetic and copies ran while one was open for 0% -> 0% of each run, Pallas kernels for 6% -> 6%
where the time goes in v3:
time: 19.9 us; the launch traced here: 19.8 us
  starting transfers between devices  11.2 us (56%)
  Pallas kernels  5.61 us (28%)
  waiting for transfers between devices  2.02 us (10%)
  other arithmetic  0.83 us (4%)
    ppermute x5, starting transfers between devices, crossed(): return lax.ppermute(v, (axis, 'cols'), pairs)  10.8 us
    pallas_call x1, Pallas kernels, fast(): pl.pallas_call(main_kernel, out_shape=jax.ShapeDtypeStruct((1, 32), F32),...  4.25 us
    ppermute x1, waiting for transfers between devices, fast(): far = lax.ppermute(near, 'cols', swap)  1.03 us
    ppermute x5, waiting for transfers between devices, crossed(): return lax.ppermute(v, (axis, 'cols'), pairs)  0.99 us
    pallas_call x1, Pallas kernels, prep(): pl.pallas_call(prep_kernel, out_shape=(jax.ShapeDtypeStruct((640, 512), B...  0.84 us
    add x1, other arithmetic, fast(): lax.pad(right_feat[0], zero, ((0, 0, 0), (0, 320, 0)))  0.83 us
    ppermute x1, starting transfers between devices, fast(): far = lax.ppermute(near, 'cols', swap)  0.41 us
  transfers between devices with their start and end apart: 7, of which 4 were waited for; matrix products, arithmetic and copies ran while one was open for 0% of the time, Pallas kernels for 6%

profile of v3, /device:TPU:0, one launch (start us, length us, event | category | flops | bytes accessed | tf_op | source)
XLA Modules:
  0.0 19.8 jit_solution(8835929685953779145)
XLA Ops:
  0.0 0.8 %pad_add_fusion.s_ref = bf16[32,640]{1,0:T(8,128)(2,1)S(1)} fusion(bf16[32,320]{1,0:T(8,128)(2,1)} %bitcast.4, bf16[32,320]{1,0:T(8,128)(2,1)} %bitcast.5), kind=kLoop, calls=%fused_computation | loop fusion | flops 81920 | bytes 81920 | tf_op jit(solution)/shard_map/add | solution.py:542
  0.8 2.4 %collective-permute-start = (bf16[32,640]{1,0:T(8,128)(2,1)S(1)}, bf16[32,640]{1,0:T(8,128)(2,1)S(1)}, u32[]{:S(2)}, u32[]{:S(2)}) collective-permute-start(bf16[32,640]{1,0:T(8,128)(2,1)S(1)} %pad_add_fusion.s_ref), channel_id=1, source_target_pairs={{0,3},{1,2},{2,1},{3,0},{4,7},{5,6},{6,5},{7,4},{8,11},{9,10},{10,... | collective-permute-start | bytes 122888 | tf_op jit(solution)/shard_map/ppermute | solution.py:537
  3.2 0.1 stage.1
  3.3 3.9 %collective-permute-start.3 = (bf16[40,320]{1,0:T(8,128)(2,1)S(1)}, bf16[40,320]{1,0:T(8,128)(2,1)S(1)}, u32[]{:S(2)}, u32[]{:S(2)}) collective-permute-start(bf16[40,320]{1,0:T(8,128)(2,1)S(1)} %stage.1), channel_id=1, source_target_pairs={{0,13},{1,12},{4,9},{5,8},{8,5},{9,4},{12,1},{13,0},{2,15},{3,14},... | collective-permute-start | bytes 76808 | tf_op jit(solution)/shard_map/ppermute | solution.py:537
  7.2 0.0 collective-permute-done.t_ref
  7.3 0.1 pack.1
  7.3 0.1 collective-permute-start.4
  7.4 0.3 %perm.1.perm_ref = bf16[640,1024]{1,0:T(8,128)(2,1)S(1)} custom-call(), custom_call_target="tpu_custom_call" | custom-call | flops 1000000000 | bytes 3000000 | tf_op jit(solution)/shard_map/perm/pallas_call | solution.py:236
  7.7 1.6 %collective-permute-start.2 = (bf16[32,640]{1,0:T(8,128)(2,1)S(1)}, bf16[32,640]{1,0:T(8,128)(2,1)S(1)}, u32[]{:S(2)}, u32[]{:S(2)}) collective-permute-start(bf16[32,640]{1,0:T(8,128)(2,1)S(1)} %get-tuple-element.27), channel_id=1, source_target_pairs={{0,9},{1,8},{4,13},{5,12},{8,1},{9,0},{12,5},{13,4},{2,11},{3,10},... | collective-permute-start | bytes 122888 | tf_op jit(solution)/shard_map/ppermute | solution.py:537
  9.3 1.3 %collective-permute-start.1 = (bf16[40,640]{1,0:T(8,128)(2,1)S(1)}, bf16[40,640]{1,0:T(8,128)(2,1)S(1)}, u32[]{:S(2)}, u32[]{:S(2)}) collective-permute-start(bf16[40,640]{1,0:T(8,128)(2,1)S(1)} %get-tuple-element.26), channel_id=1, source_target_pairs={{0,5},{1,4},{4,1},{5,0},{8,13},{9,12},{12,9},{13,8},{2,7},{3,6},{6... | collective-permute-start | bytes 153608 | tf_op jit(solution)/shard_map/ppermute | solution.py:537
  10.6 0.0 collective-permute-done.3.s_ref
  10.6 0.0 collective-permute-done.4.other
  10.6 1.5 %collective-permute-start.5 = (bf16[40,320]{1,0:T(8,128)(2,1)S(1)}, bf16[40,320]{1,0:T(8,128)(2,1)S(1)}, u32[]{:S(2)}, u32[]{:S(2)}) collective-permute-start(bf16[40,320]{1,0:T(8,128)(2,1)S(1)} %collective-permute-done.3.s_ref), channel_id=1, source_target_pairs={{0,3},{1,2},{2,1},{3,0},{4,7},{5,6},{6,5},{7,4},{8,11},{9,10},{10,... | collective-permute-start | bytes 76808 | tf_op jit(solution)/shard_map/ppermute | solution.py:537
  12.1 0.0 copy-done
  12.1 0.0 copy-done.1
  12.1 0.0 copy-done.2
  12.1 0.8 %prep.1 = (bf16[640,512]{1,0:T(8,128)(2,1)S(1)}, bf16[2,1024,512]{2,1,0:T(8,128)(2,1)S(1)}, bf16[1024,128]{1,0:T(8,128)(2,1)S(1)}) custom-call(bf16[640,1024]{1,0:T(8,128)(2,1)S(1)} %perm.1.perm_ref, bf16[27,32,40]{2,1,0:T(8,128)(2,1)S(1)} %copy-done.1, bf16[2,27,32,32]{3,2,1,0:T(8,128)(2,1)S(1)} %copy-done, bf16[27,32]{1,0:T(8,128)(2,1)S(1)} %bitcast.3), custom_call_target="tpu_custom_call" | custom-call | flops 2000000000 | bytes 4000000 | tf_op jit(solution)/shard_map/prep/pallas_call | solution.py:244
  13.0 0.4 %collective-permute-done.2.two_ref = bf16[32,640]{1,0:T(8,128)(2,1)S(1)} collective-permute-done((bf16[32,640]{1,0:T(8,128)(2,1)S(1)}, bf16[32,640]{1,0:T(8,128)(2,1)S(1)}, u32[]{:S(2)}, u32[]{:S(2)}) %collective-permute-start.2) | collective-permute-done | bytes 40992 | tf_op jit(solution)/shard_map/ppermute | solution.py:537
  13.4 0.4 %collective-permute-done.1.one_ref = bf16[40,640]{1,0:T(8,128)(2,1)S(1)} collective-permute-done((bf16[40,640]{1,0:T(8,128)(2,1)S(1)}, bf16[40,640]{1,0:T(8,128)(2,1)S(1)}, u32[]{:S(2)}, u32[]{:S(2)}) %collective-permute-start.1) | collective-permute-done | bytes 51232 | tf_op jit(solution)/shard_map/ppermute | solution.py:537
  13.8 0.1 collective-permute-done.5.t_ref
  14.0 0.1 collect.1.near
  14.1 0.4 %collective-permute-start.6 = (bf16[3,40,640]{2,1,0:T(8,128)(2,1)S(1)}, bf16[3,40,640]{2,1,0:T(8,128)(2,1)S(1)}, u32[]{:S(2)}, u32[]{:S(2)}) collective-permute-start(bf16[3,40,640]{2,1,0:T(8,128)(2,1)S(1)} %collect.1.near), channel_id=1, source_target_pairs={{0,1},{1,0},{2,3},{3,2},{4,5},{5,4},{6,7},{7,6},{8,9},{9,8},{10,11... | collective-permute-start | bytes 460808 | tf_op jit(solution)/shard_map/ppermute | solution.py:559
  14.5 1.0 %collective-permute-done.6.far = bf16[3,40,640]{2,1,0:T(8,128)(2,1)S(1)} collective-permute-done((bf16[3,40,640]{2,1,0:T(8,128)(2,1)S(1)}, bf16[3,40,640]{2,1,0:T(8,128)(2,1)S(1)}, u32[]{:S(2)}, u32[]{:S(2)}) %collective-permute-start.6) | collective-permute-done | bytes 153632 | tf_op jit(solution)/shard_map/ppermute | solution.py:559
  15.5 4.3 %cost_volume.1 = f32[1,32]{1,0:T(1,128)} custom-call(bf16[64,640]{1,0:T(8,128)(2,1)S(1)} %get-tuple-element.22.own, bf16[64,640]{1,0:T(8,128)(2,1)S(1)} %collective-permute-done.4.other, bf16[3,40,640]{2,1,0:T(8,128)(2,1)S(1)} %collect.1.near, bf16[3,40,640]{2,1,0:T(8,128)(2,1)S(1)} %collective-permute-done.6.far, ...), custom_call_target="tpu_custom_call" | custom-call | tf_op jit(solution)/shard_map/cost_volume/pallas_call | solution.py:561
  (3 shorter events, 0.0 us)
Async XLA Ops:
  0.8 6.4 %collective-permute-start = (bf16[32,640]{1,0:T(8,128)(2,1)S(1)}, bf16[32,640]{1,0:T(8,128)(2,1)S(1)}, u32[]{:S(2)}, u32[]{:S(2)}) collective-permute-start(bf16[32,640]{1,0:T(8,128)(2,1)S(1)} %pad_add_fusion.s_ref), channel_id=1, source_target_pairs={{0,3},{1,2},{2,1},{3,0},{4,7},{5,6},{6,5},{7,4},{8,11},{9,10},{10,... | collective-permute-start | bytes 122888 | tf_op jit(solution)/shard_map/ppermute | solution.py:537
  3.3 8.8 %copy-start = (bf16[2,27,32,32]{3,2,1,0:T(8,128)(2,1)S(1)}, bf16[2,27,32,32]{3,2,1,0:T(8,128)(2,1)}, u32[]{:S(2)}) copy-start(bf16[2,27,32,32]{3,2,1,0:T(8,128)(2,1)} %cm_ref.1) | copy-start | bytes 331780
  3.3 8.8 %copy-start.1 = (bf16[27,32,40]{2,1,0:T(8,128)(2,1)S(1)}, bf16[27,32,40]{2,1,0:T(8,128)(2,1)}, u32[]{:S(2)}) copy-start(bf16[27,32,40]{2,1,0:T(8,128)(2,1)} %cf_ref.1) | copy-start | bytes 207364
  3.3 8.8 %copy-start.2 = (bf16[27,1,32]{2,0,1:T(8,128)(2,1)S(1)}, bf16[27,1,32]{2,0,1:T(8,128)(2,1)}, u32[]{:S(2)}) copy-start(bf16[27,1,32]{2,0,1:T(8,128)(2,1)} %param.9) | copy-start | bytes 5188
  3.3 7.3 %collective-permute-start.3 = (bf16[40,320]{1,0:T(8,128)(2,1)S(1)}, bf16[40,320]{1,0:T(8,128)(2,1)S(1)}, u32[]{:S(2)}, u32[]{:S(2)}) collective-permute-start(bf16[40,320]{1,0:T(8,128)(2,1)S(1)} %stage.1), channel_id=1, source_target_pairs={{0,13},{1,12},{4,9},{5,8},{8,5},{9,4},{12,1},{13,0},{2,15},{3,14},... | collective-permute-start | bytes 76808 | tf_op jit(solution)/shard_map/ppermute | solution.py:537
  7.3 3.3 %collective-permute-start.4 = (bf16[64,640]{1,0:T(8,128)(2,1)S(1)}, bf16[64,640]{1,0:T(8,128)(2,1)S(1)}, u32[]{:S(2)}, u32[]{:S(2)}) collective-permute-start(bf16[64,640]{1,0:T(8,128)(2,1)S(1)} %get-tuple-element.22.own), channel_id=1, source_target_pairs={{0,1},{1,0},{2,3},{3,2},{4,5},{5,4},{6,7},{7,6},{8,9},{9,8},{10,11... | collective-permute-start | bytes 245768 | tf_op jit(solution)/shard_map/ppermute | solution.py:551
  7.7 5.7 %collective-permute-start.2 = (bf16[32,640]{1,0:T(8,128)(2,1)S(1)}, bf16[32,640]{1,0:T(8,128)(2,1)S(1)}, u32[]{:S(2)}, u32[]{:S(2)}) collective-permute-start(bf16[32,640]{1,0:T(8,128)(2,1)S(1)} %get-tuple-element.27), channel_id=1, source_target_pairs={{0,9},{1,8},{4,13},{5,12},{8,1},{9,0},{12,5},{13,4},{2,11},{3,10},... | collective-permute-start | bytes 122888 | tf_op jit(solution)/shard_map/ppermute | solution.py:537
  9.3 4.5 %collective-permute-start.1 = (bf16[40,640]{1,0:T(8,128)(2,1)S(1)}, bf16[40,640]{1,0:T(8,128)(2,1)S(1)}, u32[]{:S(2)}, u32[]{:S(2)}) collective-permute-start(bf16[40,640]{1,0:T(8,128)(2,1)S(1)} %get-tuple-element.26), channel_id=1, source_target_pairs={{0,5},{1,4},{4,1},{5,0},{8,13},{9,12},{12,9},{13,8},{2,7},{3,6},{6... | collective-permute-start | bytes 153608 | tf_op jit(solution)/shard_map/ppermute | solution.py:537
  10.6 3.3 %collective-permute-start.5 = (bf16[40,320]{1,0:T(8,128)(2,1)S(1)}, bf16[40,320]{1,0:T(8,128)(2,1)S(1)}, u32[]{:S(2)}, u32[]{:S(2)}) collective-permute-start(bf16[40,320]{1,0:T(8,128)(2,1)S(1)} %collective-permute-done.3.s_ref), channel_id=1, source_target_pairs={{0,3},{1,2},{2,1},{3,0},{4,7},{5,6},{6,5},{7,4},{8,11},{9,10},{10,... | collective-permute-start | bytes 76808 | tf_op jit(solution)/shard_map/ppermute | solution.py:537
  14.1 1.4 %collective-permute-start.6 = (bf16[3,40,640]{2,1,0:T(8,128)(2,1)S(1)}, bf16[3,40,640]{2,1,0:T(8,128)(2,1)S(1)}, u32[]{:S(2)}, u32[]{:S(2)}) collective-permute-start(bf16[3,40,640]{2,1,0:T(8,128)(2,1)S(1)} %collect.1.near), channel_id=1, source_target_pairs={{0,1},{1,0},{2,3},{3,2},{4,5},{5,4},{6,7},{7,6},{8,9},{9,8},{10,11... | collective-permute-start | bytes 460808 | tf_op jit(solution)/shard_map/ppermute | solution.py:559

commit v4 on v3

--- a/solution.py
+++ b/solution.py
@@ -474,8 +474,11 @@
     out_ref[0] = one_ref[...]
     out_ref[1, 0:32] = two_ref[...]
     out_ref[1, 32:40] = jnp.zeros((8, 640), BF)
-    out_ref[2, :, 0:320] = s_ref[...]
-    out_ref[2, :, 320:640] = t_ref[...]
+    for half, ref in enumerate((s_ref, t_ref)):
+        lanes = slice(320 * half, 320 * half + 320)
+        left = ref[:, 320:]
+        out_ref[2, 0:32, lanes] = ref[:, :320]
+        out_ref[2, 32:40, lanes] = jnp.concatenate([left[:4], left[28:]], axis=0)
 
 
 def collect(*parts):
@@ -491,16 +494,14 @@
 
 
 def stage_kernel(s_ref, out_ref):
-    left = s_ref[:, 320:]
-    out_ref[0:32] = s_ref[:, :320]
-    out_ref[32:40] = jnp.concatenate([left[:4], left[28:]], axis=0)
+    out_ref[...] = s_ref[...]
 
 
 def stage(s):
     vm = pl.BlockSpec(memory_space=pltpu.VMEM)
     return pl.pallas_call(
         stage_kernel,
-        out_shape=jax.ShapeDtypeStruct((40, 320), BF),
+        out_shape=jax.ShapeDtypeStruct(s.shape, BF),
         in_specs=[vm],
         out_specs=vm,
         compiler_params=pltpu.CompilerParams(vmem_limit_bytes=2**20),
@@ -548,10 +549,9 @@
     swap = [(0, 1), (1, 0)]
     from_1 = crossed(edge, "disp", 1)
     from_2 = crossed(rights, "disp", 2)
-    other = lax.ppermute(own, "cols", swap)
-    s_3, other = lax.optimization_barrier((s_3, other))
     t_3 = crossed(s_3, "rows", 1)
     ws = prep(conv_first, conv_mid, conv_last.reshape(27, 32))
+    other = lax.ppermute(own, "cols", swap)
     ws, from_1, from_2, s_3, t_3, other = lax.optimization_barrier(
         (ws, from_1, from_2, s_3, t_3, other)
     )

time: 19.9 us -> 19.7 us (0.990)
    ppermute x5, starting transfers between devices: 10.8 us -> 10.5 us  [crossed(): return lax.ppermute(v, (axis, 'cols'), pairs)]
  transfers between devices with their start and end apart: 7 -> 7, of which waited for: 4 -> 2; matrix products, arithmetic and copies ran while one was open for 0% -> 0% of each run, Pallas kernels for 6% -> 6%
where the time goes in v4:
time: 19.7 us; the launch traced here: 19.6 us
  starting transfers between devices  11.1 us (56%)
  Pallas kernels  5.54 us (28%)
  waiting for transfers between devices  2.03 us (10%)
  other arithmetic  0.83 us (4%)
    ppermute x5, starting transfers between devices, crossed(): return lax.ppermute(v, (axis, 'cols'), pairs)  10.5 us
    pallas_call x1, Pallas kernels, fast(): pl.pallas_call(main_kernel, out_shape=jax.ShapeDtypeStruct((1, 32), F32),...  4.25 us
    ppermute x1, waiting for transfers between devices, fast(): far = lax.ppermute(near, 'cols', swap)  1.02 us
    ppermute x5, waiting for transfers between devices, crossed(): return lax.ppermute(v, (axis, 'cols'), pairs)  1.01 us
    pallas_call x1, Pallas kernels, prep(): pl.pallas_call(prep_kernel, out_shape=(jax.ShapeDtypeStruct((640, 512), B...  0.84 us
    add x1, other arithmetic, fast(): lax.pad(right_feat[0], zero, ((0, 0, 0), (0, 320, 0)))  0.83 us
    ppermute x1, starting transfers between devices, fast(): far = lax.ppermute(near, 'cols', swap)  0.51 us
  transfers between devices with their start and end apart: 7, of which 2 were waited for; matrix products, arithmetic and copies ran while one was open for 0% of the time, Pallas kernels for 6%

profile of v4, /device:TPU:0, one launch (start us, length us, event | category | flops | bytes accessed | tf_op | source)
XLA Modules:
  0.0 19.6 jit_solution(9819039784635996703)
XLA Ops:
  0.0 0.8 %pad_add_fusion.s_ref = bf16[32,640]{1,0:T(8,128)(2,1)S(1)} fusion(bf16[32,320]{1,0:T(8,128)(2,1)} %bitcast.4, bf16[32,320]{1,0:T(8,128)(2,1)} %bitcast.5), kind=kLoop, calls=%fused_computation | loop fusion | flops 81920 | bytes 81920 | tf_op jit(solution)/shard_map/add | solution.py:543
  0.8 2.4 %collective-permute-start = (bf16[32,640]{1,0:T(8,128)(2,1)S(1)}, bf16[32,640]{1,0:T(8,128)(2,1)S(1)}, u32[]{:S(2)}, u32[]{:S(2)}) collective-permute-start(bf16[32,640]{1,0:T(8,128)(2,1)S(1)} %pad_add_fusion.s_ref), channel_id=1, source_target_pairs={{0,3},{1,2},{2,1},{3,0},{4,7},{5,6},{6,5},{7,4},{8,11},{9,10},{10,... | collective-permute-start | bytes 122888 | tf_op jit(solution)/shard_map/ppermute | solution.py:538
  3.2 0.0 copy-start.2
  3.2 3.9 %collective-permute-start.3 = (bf16[32,640]{1,0:T(8,128)(2,1)S(1)}, bf16[32,640]{1,0:T(8,128)(2,1)S(1)}, u32[]{:S(2)}, u32[]{:S(2)}) collective-permute-start(bf16[32,640]{1,0:T(8,128)(2,1)S(1)} %stage.1), channel_id=1, source_target_pairs={{0,13},{1,12},{4,9},{5,8},{8,5},{9,4},{12,1},{13,0},{2,15},{3,14},... | collective-permute-start | bytes 122888 | tf_op jit(solution)/shard_map/ppermute | solution.py:538
  7.2 0.3 %perm.1.perm_ref = bf16[640,1024]{1,0:T(8,128)(2,1)S(1)} custom-call(), custom_call_target="tpu_custom_call" | custom-call | flops 1000000000 | bytes 3000000 | tf_op jit(solution)/shard_map/perm/pallas_call | solution.py:236
  7.5 0.0 collective-permute-done.t_ref
  7.5 0.1 pack.1
  7.6 1.0 %collective-permute-start.2 = (bf16[32,640]{1,0:T(8,128)(2,1)S(1)}, bf16[32,640]{1,0:T(8,128)(2,1)S(1)}, u32[]{:S(2)}, u32[]{:S(2)}) collective-permute-start(bf16[32,640]{1,0:T(8,128)(2,1)S(1)} %get-tuple-element.25), channel_id=1, source_target_pairs={{0,9},{1,8},{4,13},{5,12},{8,1},{9,0},{12,5},{13,4},{2,11},{3,10},... | collective-permute-start | bytes 122888 | tf_op jit(solution)/shard_map/ppermute | solution.py:538
  8.6 1.6 %collective-permute-start.1 = (bf16[40,640]{1,0:T(8,128)(2,1)S(1)}, bf16[40,640]{1,0:T(8,128)(2,1)S(1)}, u32[]{:S(2)}, u32[]{:S(2)}) collective-permute-start(bf16[40,640]{1,0:T(8,128)(2,1)S(1)} %get-tuple-element.24), channel_id=1, source_target_pairs={{0,5},{1,4},{4,1},{5,0},{8,13},{9,12},{12,9},{13,8},{2,7},{3,6},{6... | collective-permute-start | bytes 153608 | tf_op jit(solution)/shard_map/ppermute | solution.py:538
  10.2 0.1 collective-permute-start.5
  10.3 0.0 collective-permute-done.3.s_ref
  10.3 1.6 %collective-permute-start.4 = (bf16[32,640]{1,0:T(8,128)(2,1)S(1)}, bf16[32,640]{1,0:T(8,128)(2,1)S(1)}, u32[]{:S(2)}, u32[]{:S(2)}) collective-permute-start(bf16[32,640]{1,0:T(8,128)(2,1)S(1)} %collective-permute-done.3.s_ref), channel_id=1, source_target_pairs={{0,3},{1,2},{2,1},{3,0},{4,7},{5,6},{6,5},{7,4},{8,11},{9,10},{10,... | collective-permute-start | bytes 122888 | tf_op jit(solution)/shard_map/ppermute | solution.py:538
  11.8 0.0 copy-done
  11.8 0.0 copy-done.1
  11.8 0.0 copy-done.2
  11.8 0.8 %prep.1 = (bf16[640,512]{1,0:T(8,128)(2,1)S(1)}, bf16[2,1024,512]{2,1,0:T(8,128)(2,1)S(1)}, bf16[1024,128]{1,0:T(8,128)(2,1)S(1)}) custom-call(bf16[640,1024]{1,0:T(8,128)(2,1)S(1)} %perm.1.perm_ref, bf16[27,32,40]{2,1,0:T(8,128)(2,1)S(1)} %copy-done.1, bf16[2,27,32,32]{3,2,1,0:T(8,128)(2,1)S(1)} %copy-done, bf16[27,32]{1,0:T(8,128)(2,1)S(1)} %bitcast.3), custom_call_target="tpu_custom_call" | custom-call | flops 2000000000 | bytes 4000000 | tf_op jit(solution)/shard_map/prep/pallas_call | solution.py:244
  12.7 1.0 %collective-permute-done.4.t_ref = bf16[32,640]{1,0:T(8,128)(2,1)S(1)} collective-permute-done((bf16[32,640]{1,0:T(8,128)(2,1)S(1)}, bf16[32,640]{1,0:T(8,128)(2,1)S(1)}, u32[]{:S(2)}, u32[]{:S(2)}) %collective-permute-start.4) | collective-permute-done | bytes 40992 | tf_op jit(solution)/shard_map/ppermute | solution.py:538
  13.7 0.0 collective-permute-done.2.two_ref
  13.7 0.0 collective-permute-done.1.one_ref
  13.7 0.0 collective-permute-done.5.other
  13.7 0.1 collect.1.near
  13.8 0.5 %collective-permute-start.6 = (bf16[3,40,640]{2,1,0:T(8,128)(2,1)S(1)}, bf16[3,40,640]{2,1,0:T(8,128)(2,1)S(1)}, u32[]{:S(2)}, u32[]{:S(2)}) collective-permute-start(bf16[3,40,640]{2,1,0:T(8,128)(2,1)S(1)} %collect.1.near), channel_id=1, source_target_pairs={{0,1},{1,0},{2,3},{3,2},{4,5},{5,4},{6,7},{7,6},{8,9},{9,8},{10,11... | collective-permute-start | bytes 460808 | tf_op jit(solution)/shard_map/ppermute | solution.py:559
  14.3 1.0 %collective-permute-done.6.far = bf16[3,40,640]{2,1,0:T(8,128)(2,1)S(1)} collective-permute-done((bf16[3,40,640]{2,1,0:T(8,128)(2,1)S(1)}, bf16[3,40,640]{2,1,0:T(8,128)(2,1)S(1)}, u32[]{:S(2)}, u32[]{:S(2)}) %collective-permute-start.6) | collective-permute-done | bytes 153632 | tf_op jit(solution)/shard_map/ppermute | solution.py:559
  15.3 4.3 %cost_volume.1 = f32[1,32]{1,0:T(1,128)} custom-call(bf16[64,640]{1,0:T(8,128)(2,1)S(1)} %get-tuple-element.20.own, bf16[64,640]{1,0:T(8,128)(2,1)S(1)} %collective-permute-done.5.other, bf16[3,40,640]{2,1,0:T(8,128)(2,1)S(1)} %collect.1.near, bf16[3,40,640]{2,1,0:T(8,128)(2,1)S(1)} %collective-permute-done.6.far, ...), custom_call_target="tpu_custom_call" | custom-call | tf_op jit(solution)/shard_map/cost_volume/pallas_call | solution.py:561
  (3 shorter events, 0.0 us)
Async XLA Ops:
  0.8 6.6 %collective-permute-start = (bf16[32,640]{1,0:T(8,128)(2,1)S(1)}, bf16[32,640]{1,0:T(8,128)(2,1)S(1)}, u32[]{:S(2)}, u32[]{:S(2)}) collective-permute-start(bf16[32,640]{1,0:T(8,128)(2,1)S(1)} %pad_add_fusion.s_ref), channel_id=1, source_target_pairs={{0,3},{1,2},{2,1},{3,0},{4,7},{5,6},{6,5},{7,4},{8,11},{9,10},{10,... | collective-permute-start | bytes 122888 | tf_op jit(solution)/shard_map/ppermute | solution.py:538
  3.2 8.6 %copy-start = (bf16[2,27,32,32]{3,2,1,0:T(8,128)(2,1)S(1)}, bf16[2,27,32,32]{3,2,1,0:T(8,128)(2,1)}, u32[]{:S(2)}) copy-start(bf16[2,27,32,32]{3,2,1,0:T(8,128)(2,1)} %cm_ref.1) | copy-start | bytes 331780
  3.2 8.6 %copy-start.1 = (bf16[27,32,40]{2,1,0:T(8,128)(2,1)S(1)}, bf16[27,32,40]{2,1,0:T(8,128)(2,1)}, u32[]{:S(2)}) copy-start(bf16[27,32,40]{2,1,0:T(8,128)(2,1)} %cf_ref.1) | copy-start | bytes 207364
  3.2 8.6 %copy-start.2 = (bf16[27,1,32]{2,0,1:T(8,128)(2,1)S(1)}, bf16[27,1,32]{2,0,1:T(8,128)(2,1)}, u32[]{:S(2)}) copy-start(bf16[27,1,32]{2,0,1:T(8,128)(2,1)} %param.9) | copy-start | bytes 5188
  3.2 7.0 %collective-permute-start.3 = (bf16[32,640]{1,0:T(8,128)(2,1)S(1)}, bf16[32,640]{1,0:T(8,128)(2,1)S(1)}, u32[]{:S(2)}, u32[]{:S(2)}) collective-permute-start(bf16[32,640]{1,0:T(8,128)(2,1)S(1)} %stage.1), channel_id=1, source_target_pairs={{0,13},{1,12},{4,9},{5,8},{8,5},{9,4},{12,1},{13,0},{2,15},{3,14},... | collective-permute-start | bytes 122888 | tf_op jit(solution)/shard_map/ppermute | solution.py:538
  7.6 6.1 %collective-permute-start.2 = (bf16[32,640]{1,0:T(8,128)(2,1)S(1)}, bf16[32,640]{1,0:T(8,128)(2,1)S(1)}, u32[]{:S(2)}, u32[]{:S(2)}) collective-permute-start(bf16[32,640]{1,0:T(8,128)(2,1)S(1)} %get-tuple-element.25), channel_id=1, source_target_pairs={{0,9},{1,8},{4,13},{5,12},{8,1},{9,0},{12,5},{13,4},{2,11},{3,10},... | collective-permute-start | bytes 122888 | tf_op jit(solution)/shard_map/ppermute | solution.py:538
  8.6 5.1 %collective-permute-start.1 = (bf16[40,640]{1,0:T(8,128)(2,1)S(1)}, bf16[40,640]{1,0:T(8,128)(2,1)S(1)}, u32[]{:S(2)}, u32[]{:S(2)}) collective-permute-start(bf16[40,640]{1,0:T(8,128)(2,1)S(1)} %get-tuple-element.24), channel_id=1, source_target_pairs={{0,5},{1,4},{4,1},{5,0},{8,13},{9,12},{12,9},{13,8},{2,7},{3,6},{6... | collective-permute-start | bytes 153608 | tf_op jit(solution)/shard_map/ppermute | solution.py:538
  10.2 3.5 %collective-permute-start.5 = (bf16[64,640]{1,0:T(8,128)(2,1)S(1)}, bf16[64,640]{1,0:T(8,128)(2,1)S(1)}, u32[]{:S(2)}, u32[]{:S(2)}) collective-permute-start(bf16[64,640]{1,0:T(8,128)(2,1)S(1)} %get-tuple-element.20.own), channel_id=1, source_target_pairs={{0,1},{1,0},{2,3},{3,2},{4,5},{5,4},{6,7},{7,6},{8,9},{9,8},{10,11... | collective-permute-start | bytes 245768 | tf_op jit(solution)/shard_map/ppermute | solution.py:554
  10.3 3.4 %collective-permute-start.4 = (bf16[32,640]{1,0:T(8,128)(2,1)S(1)}, bf16[32,640]{1,0:T(8,128)(2,1)S(1)}, u32[]{:S(2)}, u32[]{:S(2)}) collective-permute-start(bf16[32,640]{1,0:T(8,128)(2,1)S(1)} %collective-permute-done.3.s_ref), channel_id=1, source_target_pairs={{0,3},{1,2},{2,1},{3,0},{4,7},{5,6},{6,5},{7,4},{8,11},{9,10},{10,... | collective-permute-start | bytes 122888 | tf_op jit(solution)/shard_map/ppermute | solution.py:538
  13.8 1.5 %collective-permute-start.6 = (bf16[3,40,640]{2,1,0:T(8,128)(2,1)S(1)}, bf16[3,40,640]{2,1,0:T(8,128)(2,1)S(1)}, u32[]{:S(2)}, u32[]{:S(2)}) collective-permute-start(bf16[3,40,640]{2,1,0:T(8,128)(2,1)S(1)} %collect.1.near), channel_id=1, source_target_pairs={{0,1},{1,0},{2,3},{3,2},{4,5},{5,4},{6,7},{7,6},{8,9},{9,8},{10,11... | collective-permute-start | bytes 460808 | tf_op jit(solution)/shard_map/ppermute | solution.py:559

commit v5 on v4

--- a/solution.py
+++ b/solution.py
@@ -283,9 +283,11 @@
         for even, a, b in ((0, straight, turned), (1, turned, straight)):
             near_half.append(jnp.where(halfway, a[:128], 0.0).astype(BF))
             far_half.append(jnp.where(halfway, 0.0, b[:128]).astype(BF))
-            lp[2 * tile + even] = jnp.where(halfway[:64], a[128:], b[128:])
+            lp[2 * tile + even] = jnp.where(halfway[:64], a[128:], pltpu.roll(b[128:], 63, axis=0))
     for tile in range(4):
-        lp[8 + tile] = zp[128:, 512 + 128 * tile : 640 + 128 * tile]
+        this = zp[128:, 512 + 128 * tile : 640 + 128 * tile]
+        first = (iota((64, 128), 1) // 16) % 2 == 0
+        lp[8 + tile] = jnp.where(first, this, pltpu.roll(this, 63, axis=0))
     zm = jnp.concatenate(
         [jnp.concatenate(near_half, axis=1), jnp.concatenate(far_half, axis=1)], axis=0
     )
@@ -310,12 +312,6 @@
     for tile in range(4):
         rs[8 + tile, 0:56] = rse[:, 128 * tile : 128 * tile + 128]
 
-    def left_row(tile, column):
-        for first, row in ((36, 48), (4, 16), (0, 12)):
-            if column >= first:
-                at = row + column - first
-                return lp[tile, at : at + 1]
-
     lane = iota((32, 128), 1)
     low, even = lane < 64, (lane // 16) % 2 == 0
     depth = iota((32, 128), 0)
@@ -359,29 +355,39 @@
     def around(a, b, c):
         return jnp.where(low, b, jnp.where(even, c, a))
 
-    volume = Rows(xb1, (0, 128), (256, 384), beside)
+    def spread(block, value, own_lanes, halo_lanes):
+        xb1[32 * block : 32 * block + 32, own_lanes : own_lanes + 128] = value
+        if block > 0:
+            xb1[32 * block - 32 : 32 * block, halo_lanes : halo_lanes + 64] = value[:, :64]
+        if block < 19:
+            xb1[32 * block + 32 : 32 * block + 64, halo_lanes + 64 : halo_lanes + 128] = value[:, 64:]
+
+    for halo in (256, 384):
+        xb1[0:32, halo + 64 : halo + 128] = nothing[:, :64]
+        xb1[608:640, halo : halo + 64] = nothing[:, :64]
+    rests = {}
+    for phase in range(8):
+        group = range(phase, 20, 8)
+        base = 20 - group[-1]
+        count = 24 + 8 * len(group)
+        ats = [8 * (len(group) - 1 - index) for index in range(len(group))]
+        sums = [[None, None, None] for _ in group]
+        for c in range(12):
+            for dd in range(2 if c < 8 else 1):
+                right = rs[c, 56 * dd + base : 56 * dd + base + count]
+                for w2, at, acc in zip(group, ats, sums):
+                    left = lp[c, 12 + 2 * w2 : 13 + 2 * w2]
+                    term = left * right[at : at + 32]
+                    which = dd if c < 8 else 2
+                    acc[which] = term if acc[which] is None else acc[which] + term
+        for w2, acc in zip(group, sums):
+            spread(w2, (acc[0] * 0.125).astype(BF), 0, 256)
+            spread(w2, (acc[1] * 0.125).astype(BF), 128, 384)
+            rests[w2] = ((acc[2] + pltpu.roll(acc[2], 64, axis=1)) * 0.125).astype(BF)
     remainder = Rows(xb1, None, (512,), around)
     for w2 in range(20):
-        start = 20 - w2
-        tiles = []
-        for dd in range(2):
-            acc = None
-            for c in range(8):
-                left = jnp.where(low, left_row(c, 2 * w2), left_row(c, 2 * w2 + 1))
-                term = left * rs[c, 56 * dd + start : 56 * dd + start + 32]
-                acc = term if acc is None else acc + term
-            tiles.append(acc * 0.125)
-        acc = None
-        for c in range(4):
-            left = jnp.where(even, left_row(8 + c, 2 * w2), left_row(8 + c, 2 * w2 + 1))
-            term = left * rs[8 + c, start : start + 32]
-            acc = term if acc is None else acc + term
-        rest = (acc + pltpu.roll(acc, 64, axis=1)) * 0.125
-        volume.push(w2, [tile.astype(BF) for tile in tiles])
-        remainder.push(w2, [rest.astype(BF)])
-    volume.end()
+        remainder.push(w2, [rests[w2]])
     remainder.end()
-
 
     class Layer:
         def __init__(self, x, weights, out, cuts):

time: 19.7 us -> 19.7 us (level)
  no operation moved by 1% of the time
where the time goes in v5:
time: 19.7 us; the launch traced here: 19.5 us
  starting transfers between devices  11.1 us (56%)
  Pallas kernels  5.49 us (28%)
  waiting for transfers between devices  2.03 us (10%)
  other arithmetic  0.83 us (4%)
    ppermute x5, starting transfers between devices, crossed(): return lax.ppermute(v, (axis, 'cols'), pairs)  10.5 us
    pallas_call x1, Pallas kernels, fast(): pl.pallas_call(main_kernel, out_shape=jax.ShapeDtypeStruct((1, 32), F32),...  4.2 us
    ppermute x1, waiting for transfers between devices, fast(): far = lax.ppermute(near, 'cols', swap)  1.02 us
    ppermute x5, waiting for transfers between devices, crossed(): return lax.ppermute(v, (axis, 'cols'), pairs)  1.01 us
    pallas_call x1, Pallas kernels, prep(): pl.pallas_call(prep_kernel, out_shape=(jax.ShapeDtypeStruct((640, 512), B...  0.84 us
    add x1, other arithmetic, fast(): lax.pad(right_feat[0], zero, ((0, 0, 0), (0, 320, 0)))  0.83 us
    ppermute x1, starting transfers between devices, fast(): far = lax.ppermute(near, 'cols', swap)  0.51 us
  transfers between devices with their start and end apart: 7, of which 2 were waited for; matrix products, arithmetic and copies ran while one was open for 0% of the time, Pallas kernels for 6%

profile of v5, /device:TPU:0, one launch (start us, length us, event | category | flops | bytes accessed | tf_op | source)
XLA Modules:
  0.0 19.5 jit_solution(17885219444118712565)
XLA Ops:
  0.0 0.8 %pad_add_fusion.s_ref = bf16[32,640]{1,0:T(8,128)(2,1)S(1)} fusion(bf16[32,320]{1,0:T(8,128)(2,1)} %bitcast.4, bf16[32,320]{1,0:T(8,128)(2,1)} %bitcast.5), kind=kLoop, calls=%fused_computation | loop fusion | flops 81920 | bytes 81920 | tf_op jit(solution)/shard_map/add | solution.py:549
  0.8 2.4 %collective-permute-start = (bf16[32,640]{1,0:T(8,128)(2,1)S(1)}, bf16[32,640]{1,0:T(8,128)(2,1)S(1)}, u32[]{:S(2)}, u32[]{:S(2)}) collective-permute-start(bf16[32,640]{1,0:T(8,128)(2,1)S(1)} %pad_add_fusion.s_ref), channel_id=1, source_target_pairs={{0,3},{1,2},{2,1},{3,0},{4,7},{5,6},{6,5},{7,4},{8,11},{9,10},{10,... | collective-permute-start | bytes 122888 | tf_op jit(solution)/shard_map/ppermute | solution.py:544
  3.2 0.0 copy-start.2
  3.2 3.9 %collective-permute-start.3 = (bf16[32,640]{1,0:T(8,128)(2,1)S(1)}, bf16[32,640]{1,0:T(8,128)(2,1)S(1)}, u32[]{:S(2)}, u32[]{:S(2)}) collective-permute-start(bf16[32,640]{1,0:T(8,128)(2,1)S(1)} %stage.1), channel_id=1, source_target_pairs={{0,13},{1,12},{4,9},{5,8},{8,5},{9,4},{12,1},{13,0},{2,15},{3,14},... | collective-permute-start | bytes 122888 | tf_op jit(solution)/shard_map/ppermute | solution.py:544
  7.2 0.3 %perm.1.perm_ref = bf16[640,1024]{1,0:T(8,128)(2,1)S(1)} custom-call(), custom_call_target="tpu_custom_call" | custom-call | flops 1000000000 | bytes 3000000 | tf_op jit(solution)/shard_map/perm/pallas_call | solution.py:236
  7.5 0.0 collective-permute-done.t_ref
  7.5 0.1 pack.1
  7.6 1.0 %collective-permute-start.2 = (bf16[32,640]{1,0:T(8,128)(2,1)S(1)}, bf16[32,640]{1,0:T(8,128)(2,1)S(1)}, u32[]{:S(2)}, u32[]{:S(2)}) collective-permute-start(bf16[32,640]{1,0:T(8,128)(2,1)S(1)} %get-tuple-element.25), channel_id=1, source_target_pairs={{0,9},{1,8},{4,13},{5,12},{8,1},{9,0},{12,5},{13,4},{2,11},{3,10},... | collective-permute-start | bytes 122888 | tf_op jit(solution)/shard_map/ppermute | solution.py:544
  8.6 1.6 %collective-permute-start.1 = (bf16[40,640]{1,0:T(8,128)(2,1)S(1)}, bf16[40,640]{1,0:T(8,128)(2,1)S(1)}, u32[]{:S(2)}, u32[]{:S(2)}) collective-permute-start(bf16[40,640]{1,0:T(8,128)(2,1)S(1)} %get-tuple-element.24), channel_id=1, source_target_pairs={{0,5},{1,4},{4,1},{5,0},{8,13},{9,12},{12,9},{13,8},{2,7},{3,6},{6... | collective-permute-start | bytes 153608 | tf_op jit(solution)/shard_map/ppermute | solution.py:544
  10.2 0.1 collective-permute-start.5
  10.3 0.0 collective-permute-done.3.s_ref
  10.3 1.6 %collective-permute-start.4 = (bf16[32,640]{1,0:T(8,128)(2,1)S(1)}, bf16[32,640]{1,0:T(8,128)(2,1)S(1)}, u32[]{:S(2)}, u32[]{:S(2)}) collective-permute-start(bf16[32,640]{1,0:T(8,128)(2,1)S(1)} %collective-permute-done.3.s_ref), channel_id=1, source_target_pairs={{0,3},{1,2},{2,1},{3,0},{4,7},{5,6},{6,5},{7,4},{8,11},{9,10},{10,... | collective-permute-start | bytes 122888 | tf_op jit(solution)/shard_map/ppermute | solution.py:544
  11.8 0.0 copy-done
  11.8 0.0 copy-done.1
  11.8 0.0 copy-done.2
  11.8 0.8 %prep.1 = (bf16[640,512]{1,0:T(8,128)(2,1)S(1)}, bf16[2,1024,512]{2,1,0:T(8,128)(2,1)S(1)}, bf16[1024,128]{1,0:T(8,128)(2,1)S(1)}) custom-call(bf16[640,1024]{1,0:T(8,128)(2,1)S(1)} %perm.1.perm_ref, bf16[27,32,40]{2,1,0:T(8,128)(2,1)S(1)} %copy-done.1, bf16[2,27,32,32]{3,2,1,0:T(8,128)(2,1)S(1)} %copy-done, bf16[27,32]{1,0:T(8,128)(2,1)S(1)} %bitcast.3), custom_call_target="tpu_custom_call" | custom-call | flops 2000000000 | bytes 4000000 | tf_op jit(solution)/shard_map/prep/pallas_call | solution.py:244
  12.7 1.0 %collective-permute-done.4.t_ref = bf16[32,640]{1,0:T(8,128)(2,1)S(1)} collective-permute-done((bf16[32,640]{1,0:T(8,128)(2,1)S(1)}, bf16[32,640]{1,0:T(8,128)(2,1)S(1)}, u32[]{:S(2)}, u32[]{:S(2)}) %collective-permute-start.4) | collective-permute-done | bytes 40992 | tf_op jit(solution)/shard_map/ppermute | solution.py:544
  13.7 0.0 collective-permute-done.2.two_ref
  13.7 0.0 collective-permute-done.1.one_ref
  13.7 0.0 collective-permute-done.5.other
  13.7 0.1 collect.1.near
  13.8 0.5 %collective-permute-start.6 = (bf16[3,40,640]{2,1,0:T(8,128)(2,1)S(1)}, bf16[3,40,640]{2,1,0:T(8,128)(2,1)S(1)}, u32[]{:S(2)}, u32[]{:S(2)}) collective-permute-start(bf16[3,40,640]{2,1,0:T(8,128)(2,1)S(1)} %collect.1.near), channel_id=1, source_target_pairs={{0,1},{1,0},{2,3},{3,2},{4,5},{5,4},{6,7},{7,6},{8,9},{9,8},{10,11... | collective-permute-start | bytes 460808 | tf_op jit(solution)/shard_map/ppermute | solution.py:565
  14.3 1.0 %collective-permute-done.6.far = bf16[3,40,640]{2,1,0:T(8,128)(2,1)S(1)} collective-permute-done((bf16[3,40,640]{2,1,0:T(8,128)(2,1)S(1)}, bf16[3,40,640]{2,1,0:T(8,128)(2,1)S(1)}, u32[]{:S(2)}, u32[]{:S(2)}) %collective-permute-start.6) | collective-permute-done | bytes 153632 | tf_op jit(solution)/shard_map/ppermute | solution.py:565
  15.3 4.2 %cost_volume.1 = f32[1,32]{1,0:T(1,128)} custom-call(bf16[64,640]{1,0:T(8,128)(2,1)S(1)} %get-tuple-element.20.own, bf16[64,640]{1,0:T(8,128)(2,1)S(1)} %collective-permute-done.5.other, bf16[3,40,640]{2,1,0:T(8,128)(2,1)S(1)} %collect.1.near, bf16[3,40,640]{2,1,0:T(8,128)(2,1)S(1)} %collective-permute-done.6.far, ...), custom_call_target="tpu_custom_call" | custom-call | tf_op jit(solution)/shard_map/cost_volume/pallas_call | solution.py:567
  (3 shorter events, 0.0 us)
Async XLA Ops:
  0.8 6.6 %collective-permute-start = (bf16[32,640]{1,0:T(8,128)(2,1)S(1)}, bf16[32,640]{1,0:T(8,128)(2,1)S(1)}, u32[]{:S(2)}, u32[]{:S(2)}) collective-permute-start(bf16[32,640]{1,0:T(8,128)(2,1)S(1)} %pad_add_fusion.s_ref), channel_id=1, source_target_pairs={{0,3},{1,2},{2,1},{3,0},{4,7},{5,6},{6,5},{7,4},{8,11},{9,10},{10,... | collective-permute-start | bytes 122888 | tf_op jit(solution)/shard_map/ppermute | solution.py:544
  3.2 8.6 %copy-start = (bf16[2,27,32,32]{3,2,1,0:T(8,128)(2,1)S(1)}, bf16[2,27,32,32]{3,2,1,0:T(8,128)(2,1)}, u32[]{:S(2)}) copy-start(bf16[2,27,32,32]{3,2,1,0:T(8,128)(2,1)} %cm_ref.1) | copy-start | bytes 331780
  3.2 8.6 %copy-start.1 = (bf16[27,32,40]{2,1,0:T(8,128)(2,1)S(1)}, bf16[27,32,40]{2,1,0:T(8,128)(2,1)}, u32[]{:S(2)}) copy-start(bf16[27,32,40]{2,1,0:T(8,128)(2,1)} %cf_ref.1) | copy-start | bytes 207364
  3.2 8.6 %copy-start.2 = (bf16[27,1,32]{2,0,1:T(8,128)(2,1)S(1)}, bf16[27,1,32]{2,0,1:T(8,128)(2,1)}, u32[]{:S(2)}) copy-start(bf16[27,1,32]{2,0,1:T(8,128)(2,1)} %param.9) | copy-start | bytes 5188
  3.2 7.0 %collective-permute-start.3 = (bf16[32,640]{1,0:T(8,128)(2,1)S(1)}, bf16[32,640]{1,0:T(8,128)(2,1)S(1)}, u32[]{:S(2)}, u32[]{:S(2)}) collective-permute-start(bf16[32,640]{1,0:T(8,128)(2,1)S(1)} %stage.1), channel_id=1, source_target_pairs={{0,13},{1,12},{4,9},{5,8},{8,5},{9,4},{12,1},{13,0},{2,15},{3,14},... | collective-permute-start | bytes 122888 | tf_op jit(solution)/shard_map/ppermute | solution.py:544
  7.6 6.1 %collective-permute-start.2 = (bf16[32,640]{1,0:T(8,128)(2,1)S(1)}, bf16[32,640]{1,0:T(8,128)(2,1)S(1)}, u32[]{:S(2)}, u32[]{:S(2)}) collective-permute-start(bf16[32,640]{1,0:T(8,128)(2,1)S(1)} %get-tuple-element.25), channel_id=1, source_target_pairs={{0,9},{1,8},{4,13},{5,12},{8,1},{9,0},{12,5},{13,4},{2,11},{3,10},... | collective-permute-start | bytes 122888 | tf_op jit(solution)/shard_map/ppermute | solution.py:544
  8.6 5.1 %collective-permute-start.1 = (bf16[40,640]{1,0:T(8,128)(2,1)S(1)}, bf16[40,640]{1,0:T(8,128)(2,1)S(1)}, u32[]{:S(2)}, u32[]{:S(2)}) collective-permute-start(bf16[40,640]{1,0:T(8,128)(2,1)S(1)} %get-tuple-element.24), channel_id=1, source_target_pairs={{0,5},{1,4},{4,1},{5,0},{8,13},{9,12},{12,9},{13,8},{2,7},{3,6},{6... | collective-permute-start | bytes 153608 | tf_op jit(solution)/shard_map/ppermute | solution.py:544
  10.2 3.5 %collective-permute-start.5 = (bf16[64,640]{1,0:T(8,128)(2,1)S(1)}, bf16[64,640]{1,0:T(8,128)(2,1)S(1)}, u32[]{:S(2)}, u32[]{:S(2)}) collective-permute-start(bf16[64,640]{1,0:T(8,128)(2,1)S(1)} %get-tuple-element.20.own), channel_id=1, source_target_pairs={{0,1},{1,0},{2,3},{3,2},{4,5},{5,4},{6,7},{7,6},{8,9},{9,8},{10,11... | collective-permute-start | bytes 245768 | tf_op jit(solution)/shard_map/ppermute | solution.py:560
  10.3 3.4 %collective-permute-start.4 = (bf16[32,640]{1,0:T(8,128)(2,1)S(1)}, bf16[32,640]{1,0:T(8,128)(2,1)S(1)}, u32[]{:S(2)}, u32[]{:S(2)}) collective-permute-start(bf16[32,640]{1,0:T(8,128)(2,1)S(1)} %collective-permute-done.3.s_ref), channel_id=1, source_target_pairs={{0,3},{1,2},{2,1},{3,0},{4,7},{5,6},{6,5},{7,4},{8,11},{9,10},{10,... | collective-permute-start | bytes 122888 | tf_op jit(solution)/shard_map/ppermute | solution.py:544
  13.8 1.5 %collective-permute-start.6 = (bf16[3,40,640]{2,1,0:T(8,128)(2,1)S(1)}, bf16[3,40,640]{2,1,0:T(8,128)(2,1)S(1)}, u32[]{:S(2)}, u32[]{:S(2)}) collective-permute-start(bf16[3,40,640]{2,1,0:T(8,128)(2,1)S(1)} %collect.1.near), channel_id=1, source_target_pairs={{0,1},{1,0},{2,3},{3,2},{4,5},{5,4},{6,7},{7,6},{8,9},{9,8},{10,11... | collective-permute-start | bytes 460808 | tf_op jit(solution)/shard_map/ppermute | solution.py:565
